TPU v7x, 256 devices: a whole 4x4x8 slice. The times are simulated.
256 devices in a mesh: dp: 32 (over x_lo, z, core), expert: 8 (over x_hi, y).
Axes of the slice: x: 4 (x_hi: 2, x_lo: 2; x = x_hi * 2 + x_lo), y: 4, z: 8, core: 2. Of those that a mesh axis runs over, the one named last changes fastest.
Arguments:
- grad_out: bfloat16 [32768, 2560], P(('dp', 'expert')), may hold values from -6 to 6
- saved_input: bfloat16 [32768, 2560], P(('dp', 'expert')), may hold values from -6 to 6
- expert_ids: int32 [32768, 2], P(('dp', 'expert')), may hold values from 0 to 15, all different within a row; in each aligned block of 128 rows (0 to 127, 128 to 255, ...) at most 32 rows name the same one
- gate_weights: float32 [32768, 2], P(('dp', 'expert')), may hold values from 0.2 to 1
- up_weight: bfloat16 [16, 2560, 512], P('expert', 'dp'), may hold values from -0.125 to 0.125
- down_weight: bfloat16 [16, 512, 2560], P('expert', 'dp'), may hold values from -0.25 to 0.25
- engram_gate: float32 [32768, 4], P(('dp', 'expert')), may hold values from 0.1 to 1
- memory_owner: int32 [32768, 4], P(('dp', 'expert')), may hold values from 0 to 31, all different within a row; in each aligned block of 128 rows (0 to 127, 128 to 255, ...) at most 32 rows name the same one
- memory_slot: int32 [32768, 4], P(('dp', 'expert')), may hold values from 0 to 127
Outputs:
- grad_input: bfloat16 [32768, 2560], P(('dp', 'expert'))
- table_grad: float32 [4, 4096, 1280], P(None, ('dp', 'expert'))
Inputs may be any that keep to these rules, and one draw needn't show every extreme that they name: `expert_ids`: each row names 2 different experts; among the rows of one device (aligned blocks of 128 rows) no expert is named more than 32 times, a bound that some block reaches. `memory_owner`: each row names 4 different owners; among the rows of one device (aligned blocks of 128 rows) no owner is named more than 32 times, a bound that some block reaches.
All inputs are finite; a program needn't handle non-finite values.
Results may differ from a plain program's by a relative error of at most 0.014.
Values may be sent and summed in bfloat16 or wider, within the bound.
A program may use at most 128 MiB of HBM per device.

v0:
```python
import jax
import jax.numpy as jnp
from jax import lax
from jax.sharding import PartitionSpec as P

TOP = 2
HEADS = 2
SHARD = 128


def silu_slope(pre):
    sig = jax.nn.sigmoid(pre)
    return sig * (1.0 + pre * (1.0 - sig))


def slot_places(targets, groups, capacity):
    flat = targets.reshape(-1)
    onehot = (flat[:, None] == jnp.arange(groups, dtype=jnp.int32)[None, :]).astype(jnp.int32)
    before = jnp.cumsum(onehot, axis=0) - onehot
    place = jnp.sum(before * onehot, axis=1)
    return flat * capacity + place


def memory_path(grad_out, engram_gate, memory_owner, memory_slot):
    tok_rows = grad_out.shape[0]
    lookups = engram_gate.shape[1]
    width = grad_out.shape[1] // 2
    groups = lax.axis_size("dp")
    capacity = 2 * tok_rows * lookups // groups
    halves = grad_out.reshape(tok_rows, 2, width)
    rows = (engram_gate[:, :, None] * jnp.repeat(halves, HEADS, axis=1).astype(jnp.float32)).astype(
        jnp.bfloat16
    )
    places = slot_places(memory_owner, groups, capacity)
    keys = (jnp.arange(lookups, dtype=jnp.int32)[None, :] * SHARD + memory_slot).reshape(-1)
    send_rows = (
        jnp.zeros((groups * capacity, width), jnp.bfloat16).at[places].set(rows.reshape(-1, width))
    )
    send_keys = jnp.zeros((groups * capacity,), jnp.int32).at[places].set(keys)
    got_rows, got_keys = (
        lax.all_to_all(
            send_rows.reshape(groups, capacity, width),
            "dp",
            split_axis=0,
            concat_axis=0,
            tiled=True,
        ),
        lax.all_to_all(
            send_keys.reshape(groups, capacity), "dp", split_axis=0, concat_axis=0, tiled=True
        ),
    )
    dense = (
        jnp.zeros((lookups * SHARD, width), jnp.float32)
        .at[got_keys.reshape(-1)]
        .add(got_rows.reshape(-1, width).astype(jnp.float32))
    )
    return lax.psum_scatter(
        dense.reshape(lookups, SHARD, width).astype(jnp.bfloat16),
        "expert",
        scatter_dimension=1,
        tiled=True,
    ).astype(jnp.float32)


def per_device(
    grad_out,
    saved_input,
    expert_ids,
    gate_weights,
    up_weight,
    down_weight,
    engram_gate,
    memory_owner,
    memory_slot,
):
    tok_rows, width = grad_out.shape
    local_experts = up_weight.shape[0]
    groups = lax.axis_size("expert")
    experts = local_experts * groups
    capacity = 2 * tok_rows * TOP // experts
    places = slot_places(expert_ids, experts, capacity)
    send_grad = (
        jnp.zeros((experts * capacity, width), jnp.bfloat16)
        .at[places]
        .set(jnp.repeat(grad_out, TOP, axis=0))
    )
    send_input = (
        jnp.zeros((experts * capacity, width), jnp.bfloat16)
        .at[places]
        .set(jnp.repeat(saved_input, TOP, axis=0))
    )
    shape = (groups, local_experts, capacity, width)
    got_grad, got_input = (
        lax.all_to_all(send_grad.reshape(shape), "expert", split_axis=0, concat_axis=0, tiled=True),
        lax.all_to_all(
            send_input.reshape(shape), "expert", split_axis=0, concat_axis=0, tiled=True
        ),
    )
    pre = jnp.einsum(
        "secd,edh->sech",
        got_input,
        lax.all_gather(up_weight, "dp", axis=1, tiled=True),
        preferred_element_type=jnp.float32,
    )
    back = jnp.einsum(
        "secd,ehd->sech",
        got_grad,
        lax.all_gather(down_weight, "dp", axis=1, tiled=True),
        preferred_element_type=jnp.float32,
    )
    slope = (back * silu_slope(pre)).astype(jnp.bfloat16)
    expert_grad = jnp.einsum(
        "sech,edh->secd",
        slope,
        lax.all_gather(up_weight, "dp", axis=1, tiled=True),
        preferred_element_type=jnp.float32,
    ).astype(jnp.bfloat16)
    returned = lax.all_to_all(expert_grad, "expert", split_axis=0, concat_axis=0, tiled=True)
    picked = returned.reshape(experts * capacity, width)[places]
    weighted = gate_weights.reshape(-1, 1) * picked.astype(jnp.float32)
    grad_input = jnp.sum(weighted.reshape(tok_rows, TOP, width), axis=1).astype(jnp.bfloat16)
    table_part = memory_path(grad_out, engram_gate, memory_owner, memory_slot)
    return (grad_input, table_part)


def solution(mesh):
    return jax.shard_map(
        per_device,
        mesh=mesh,
        in_specs=(
            P(("dp", "expert"), None),
            P(("dp", "expert"), None),
            P(("dp", "expert"), None),
            P(("dp", "expert"), None),
            P("expert", "dp", None),
            P("expert", "dp", None),
            P(("dp", "expert"), None),
            P(("dp", "expert"), None),
            P(("dp", "expert"), None),
        ),
        out_specs=(P(("dp", "expert"), None), P(None, ("dp", "expert"), None)),
        check_vma=False,
    )
```

profile of v0, /device:TPU:1, one launch (start us, length us, event | category | flops | bytes accessed | tf_op | source)
XLA Modules:
  0.0 317.2 jit_solution(15579972233213541796)
XLA Ops:
  8.0 0.7 all-gather.5.cloned.1.call-update
  8.8 0.7 all-gather.3.cloned.1.call-update
  9.5 0.8 copy.61
  10.5 0.7 broadcast_multiply_fusion
  11.2 1.2 reduce-window.16
  12.4 0.2 slice_reduce_fusion
  12.8 0.8 broadcast_add_fusion
  13.6 0.1 copy.64
  13.9 2.4 scatter_custom_fusion.2
  16.4 0.7 all_to_all.21
  17.1 11.1 %all-to-all-start.3 = ((s32[32,1,32]{2,1,0:T(1,128)}), s32[32,1,32]{2,1,0:T(1,128)S(1)}, u32[]{:S(2)}, u32[]{:S(2)}) async-start(s32[32,1,32]{2,1,0:T(1,128)} %all_to_all.21), calls=%async_computation.3 | async-start | bytes 32768 | tf_op jit(solution)/shard_map/all_to_all | solution.py:48
  28.1 0.8 copy.54
  28.9 0.1 eq.54
  29.1 0.1 eq.50
  29.2 0.6 reduce-window.14
  29.8 0.2 slice_reduce_fusion.1
  30.0 0.7 broadcast_multiply_fusion.1
  30.7 0.1 copy.53
  30.9 0.1 mul.78
  31.1 1.8 broadcast_in_dim.11
  32.9 0.5 reshape.217
  33.4 4.3 %scatter_custom_fusion.1 = bf16[512,2560]{1,0:T(8,128)(2,1)} fusion(s32[256]{0:T(256)S(1)} %bitcast.93, bf16[256,2560]{1,0:T(8,128)(2,1)S(1)} %reshape.217, bf16[]{:T(256)} %constant.8.clone.1), kind=kCustom, calls=%fused_computation.27 | custom fusion | bytes 2621442 | tf_op jit(solution)/shard_map/scatter | solution.py:90
  37.7 6.5 %all-to-all-start.1 = ((bf16[8,2,32,2560]{3,2,1,0:T(8,128)(2,1)}), bf16[8,2,32,2560]{3,2,1,0:T(8,128)(2,1)}, u32[]{:S(2)}, u32[]{:S(2)}) async-start(bf16[8,2,32,2560]{3,2,1,0:T(8,128)(2,1)} %bitcast.7), calls=%async_computation.1 | async-start | bytes 5242880 | tf_op jit(solution)/shard_map/all_to_all | solution.py:95
  44.2 0.9 reshape.195
  45.1 2.4 broadcast_in_dim.14
  47.4 3.4 %convert_element_type.75 = f32[512,1280]{1,0:T(8,128)S(1)} reshape(f32[128,2,2,1280]{3,2,1,0:T(2,128)} %broadcast_in_dim.14) | data formatting | bytes 5242880 | tf_op jit(solution)/shard_map/convert_element_type | solution.py:31
  51.1 4.7 %scatter_custom_fusion.3 = bf16[1024,1280]{1,0:T(8,128)(2,1)} fusion(s32[512]{0:T(512)S(1)} %bitcast.99, f32[512,1280]{1,0:T(8,128)S(1)} %convert_element_type.75, f32[512]{0:T(512)S(1)} %mul.89, bf16[]{:T(256)} %constant.8.clone.1), kind=kCustom, calls=%fused_computation.23 | custom fusion | flops 1310720 | bytes 5244930 | tf_op jit(solution)/shard_map/scatter | solution.py:37
  55.7 36.7 %all-to-all-done.1 = bf16[8,2,32,2560]{3,2,1,0:T(8,128)(2,1)} async-done(((bf16[8,2,32,2560]{3,2,1,0:T(8,128)(2,1)}), bf16[8,2,32,2560]{3,2,1,0:T(8,128)(2,1)}, u32[]{:S(2)}, u32[]{:S(2)}) %all-to-all-start.1) | async-done | bytes 2621472 | tf_op jit(solution)/shard_map/all_to_all | solution.py:95
  92.5 5.6 %all-to-all-start.4 = ((bf16[32,32,1280]{2,1,0:T(8,128)(2,1)}), bf16[32,32,1280]{2,1,0:T(8,128)(2,1)S(1)}, u32[]{:S(2)}, u32[]{:S(2)}) async-start(bf16[32,32,1280]{2,1,0:T(8,128)(2,1)} %bitcast.90), calls=%async_computation.4 | async-start | bytes 5242880 | tf_op jit(solution)/shard_map/all_to_all | solution.py:41
  98.1 1.7 broadcast_in_dim.10
  99.8 4.1 %reshape.209 = bf16[256,2560]{1,0:T(8,128)(2,1)} reshape(bf16[128,2,2560]{2,1,0:T(2,128)(2,1)} %broadcast_in_dim.10) | data formatting | bytes 2621440 | tf_op jit(solution)/shard_map/reshape | solution.py:85
  103.9 5.1 %scatter_custom_fusion = bf16[512,2560]{1,0:T(8,128)(2,1)} fusion(s32[256]{0:T(256)S(1)} %bitcast.94, bf16[256,2560]{1,0:T(8,128)(2,1)} %reshape.209, bf16[]{:T(256)} %constant.8.clone.1), kind=kCustom, calls=%fused_computation.29 | custom fusion | bytes 2621952 | tf_op jit(solution)/shard_map/scatter | solution.py:85
  109.0 68.6 %all-to-all-done.4 = bf16[32,32,1280]{2,1,0:T(8,128)(2,1)S(1)} async-done(((bf16[32,32,1280]{2,1,0:T(8,128)(2,1)}), bf16[32,32,1280]{2,1,0:T(8,128)(2,1)S(1)}, u32[]{:S(2)}, u32[]{:S(2)}) %all-to-all-start.4) | async-done | bytes 2621472 | tf_op jit(solution)/shard_map/all_to_all | solution.py:41
  177.6 4.4 %all-to-all-start = ((bf16[8,2,32,2560]{3,2,1,0:T(8,128)(2,1)}), bf16[8,2,32,2560]{3,2,1,0:T(8,128)(2,1)}, u32[]{:S(2)}, u32[]{:S(2)}) async-start(bf16[8,2,32,2560]{3,2,1,0:T(8,128)(2,1)} %bitcast.3), calls=%async_computation | async-start | bytes 5242880 | tf_op jit(solution)/shard_map/all_to_all | solution.py:94
  182.1 0.5 broadcast.166
  182.6 0.7 reduce.7
  183.4 11.7 %scatter_custom_fusion.4 = f32[512,1280]{1,0:T(8,128)} fusion(s32[1024]{0:T(1024)S(1)} %bitcast.97, bf16[1024,1280]{1,0:T(8,128)(2,1)S(1)} %bitcast.89, f32[]{:T(128)} %constant.13.clone.1), kind=kCustom, calls=%fused_computation.6 | custom fusion | flops 2621440 | bytes 5242884 | tf_op jit(solution)/shard_map/scatter-add | solution.py:55
  195.1 2.9 convert_element_type.79
  198.1 5.8 %fusion.21 = f32[8,2,32,512]{3,2,0,1:T(8,128)} fusion(bf16[2,2560,512]{2,1,0:T(8,128)(2,1)} %all-gather.5.cloned.1.call-done, bf16[8,2,32,2560]{3,2,1,0:T(8,128)(2,1)} %all-to-all-done.1), kind=kOutput, calls=%fused_computation.21 | convolution fusion | flops 1342177280 | bytes 8912896 | tf_op jit(solution)/shard_map/secd,edh->sech/dot_general | solution.py:99
  203.9 6.0 %all-to-all-done = bf16[8,2,32,2560]{3,2,1,0:T(8,128)(2,1)} async-done(((bf16[8,2,32,2560]{3,2,1,0:T(8,128)(2,1)}), bf16[8,2,32,2560]{3,2,1,0:T(8,128)(2,1)}, u32[]{:S(2)}, u32[]{:S(2)}) %all-to-all-start) | async-done | bytes 2621472 | tf_op jit(solution)/shard_map/all_to_all | solution.py:94
  209.9 8.2 %fusion.11 = bf16[8,2,32,2560]{3,2,0,1:T(8,128)(2,1)S(1)} fusion(bf16[2,2560,512]{2,1,0:T(8,128)(2,1)} %all-gather.5.cloned.1.call-done, bf16[2,512,2560]{2,1,0:T(8,128)(2,1)} %all-gather.3.cloned.1.call-done, bf16[8,2,32,2560]{3,2,1,0:T(8,128)(2,1)} %all-to-all-done, f32[8,2,32,512]{3,2,0,1:T(8,128)} %fusion.21), kind=kOutput, calls=%fused_computation.15 | convolution fusion | flops 2688024576 | bytes 16777216 | tf_op jit(solution)/shard_map/sech,edh->secd/dot_general | solution.py:112
  218.1 1.7 copy.59
  219.8 8.6 %all-to-all-start.2 = ((bf16[8,2,32,2560]{3,2,1,0:T(8,128)(2,1)}), bf16[8,2,32,2560]{3,2,1,0:T(8,128)(2,1)S(1)}, u32[]{:S(2)}, u32[]{:S(2)}) async-start(bf16[8,2,32,2560]{3,2,1,0:T(8,128)(2,1)} %copy.59), calls=%async_computation.2 | async-start | bytes 5242880 | tf_op jit(solution)/shard_map/all_to_all | solution.py:118
  228.5 69.5 %reduce-scatter.2.cloned.1.call-done = bf16[4,16,1280]{2,1,0:T(8,128)(2,1)} async-done(((bf16[4,128,1280]{2,1,0:T(8,128)(2,1)}), bf16[4,16,1280]{2,1,0:T(8,128)(2,1)}) %reduce-scatter.2.cloned.1.call-update) | async-done | bytes 163856 | tf_op jit(solution)/shard_map/reduce_scatter | solution.py:57
  298.0 1.7 convert_element_type.81
  299.7 2.5 gather_fusion
  302.2 3.1 reshape.194
  305.3 4.5 %multiply_reduce_fusion = bf16[128,2560]{1,0:T(8,128)(2,1)} fusion(f32[128,2,2560]{2,1,0:T(2,128)S(1)} %reshape.194, f32[128,2]{1,0:T(8,128)S(1)} %copy.52), kind=kLoop, calls=%fused_computation.19 | loop fusion | flops 983040 | bytes 3277824 | tf_op jit(solution)/shard_map/reduce_sum | solution.py:121
  (36 shorter events, 1.4 us)
Async XLA Ops:
  8.0 190.1 %all-gather.5.cloned.1.call-start = ((), (), s32[]{:S(2)}) async-start(), calls=%async_computation.7 | async-start | bytes 5406720 | tf_op jit(solution)/shard_map/all_gather | solution.py:115
  8.7 201.2 %all-gather.3.cloned.1.call-start = ((), (), s32[]{:S(2)}) async-start(), calls=%async_computation.6 | async-start | bytes 5406720 | tf_op jit(solution)/shard_map/all_gather | solution.py:108
  17.1 20.6 %all-to-all-start.3 = ((s32[32,1,32]{2,1,0:T(1,128)}), s32[32,1,32]{2,1,0:T(1,128)S(1)}, u32[]{:S(2)}, u32[]{:S(2)}) async-start(s32[32,1,32]{2,1,0:T(1,128)} %all_to_all.21), calls=%async_computation.3 | async-start | bytes 32768 | tf_op jit(solution)/shard_map/all_to_all | solution.py:48
  37.7 6.5 %copy-start = (bf16[128,2560]{1,0:T(8,128)(2,1)S(1)}, bf16[128,2560]{1,0:T(8,128)(2,1)}, u32[]{:S(2)}) copy-start(bf16[128,2560]{1,0:T(8,128)(2,1)} %param.9) | copy-start | bytes 1966084
  37.7 54.8 %all-to-all-start.1 = ((bf16[8,2,32,2560]{3,2,1,0:T(8,128)(2,1)}), bf16[8,2,32,2560]{3,2,1,0:T(8,128)(2,1)}, u32[]{:S(2)}, u32[]{:S(2)}) async-start(bf16[8,2,32,2560]{3,2,1,0:T(8,128)(2,1)} %bitcast.7), calls=%async_computation.1 | async-start | bytes 5242880 | tf_op jit(solution)/shard_map/all_to_all | solution.py:95
  47.4 3.4 %copy-start.1 = (f32[128,4]{0,1:T(4,128)S(1)}, f32[128,4]{0,1:T(4,128)}, u32[]{:S(2)}) copy-start(f32[128,4]{0,1:T(4,128)} %param.15) | copy-start | bytes 6148
  92.5 85.2 %all-to-all-start.4 = ((bf16[32,32,1280]{2,1,0:T(8,128)(2,1)}), bf16[32,32,1280]{2,1,0:T(8,128)(2,1)S(1)}, u32[]{:S(2)}, u32[]{:S(2)}) async-start(bf16[32,32,1280]{2,1,0:T(8,128)(2,1)} %bitcast.90), calls=%async_computation.4 | async-start | bytes 5242880 | tf_op jit(solution)/shard_map/all_to_all | solution.py:41
  177.6 32.3 %all-to-all-start = ((bf16[8,2,32,2560]{3,2,1,0:T(8,128)(2,1)}), bf16[8,2,32,2560]{3,2,1,0:T(8,128)(2,1)}, u32[]{:S(2)}, u32[]{:S(2)}) async-start(bf16[8,2,32,2560]{3,2,1,0:T(8,128)(2,1)} %bitcast.3), calls=%async_computation | async-start | bytes 5242880 | tf_op jit(solution)/shard_map/all_to_all | solution.py:94
  182.1 116.0 %reduce-scatter.2.cloned.1.call-start = ((), (), s32[]{:S(2)}) async-start(), calls=%async_computation.8 | async-start | bytes 1474560 | tf_op jit(solution)/shard_map/reduce_scatter | solution.py:57
  219.8 8.6 %copy-start.2 = (f32[128,2]{0,1:T(2,128)S(1)}, f32[128,2]{0,1:T(2,128)}, u32[]{:S(2)}) copy-start(f32[128,2]{0,1:T(2,128)} %param.12) | copy-start | bytes 3076
  219.8 79.9 %all-to-all-start.2 = ((bf16[8,2,32,2560]{3,2,1,0:T(8,128)(2,1)}), bf16[8,2,32,2560]{3,2,1,0:T(8,128)(2,1)S(1)}, u32[]{:S(2)}, u32[]{:S(2)}) async-start(bf16[8,2,32,2560]{3,2,1,0:T(8,128)(2,1)} %copy.59), calls=%async_computation.2 | async-start | bytes 5242880 | tf_op jit(solution)/shard_map/all_to_all | solution.py:118
Sparse Core Ops, SparseCore 0:
  10.6 73.9 all-gather.4
  86.5 102.0 all-gather.2
Sparse Core Ops, SparseCore 1:
  198.2 99.8 reduce-scatter.1
where the time goes:
time: 319 us; the launch traced here: 317 us
  waiting for transfers between devices  182 us (57%)
  local copies, waits for them, and re-layouts  38.7 us (12%)
  starting transfers between devices  36.3 us (11%)
  other arithmetic  30.4 us (10%)
  between operations  15.7 us (5%)
  matrix products  13.9 us (4%)
    reduce_scatter x1, waiting for transfers between devices, memory_path(): lax.psum_scatter(dense.reshape(lookups, SHARD, width).astype(jnp.bfloat16...  69.5 us
    all_to_all x1, waiting for transfers between devices, memory_path(): lax.all_to_all(send_rows.reshape(groups, capacity, width), 'dp', split_ax...  68.6 us
    all_to_all x1, waiting for transfers between devices, per_device(): lax.all_to_all(send_input.reshape(shape), 'expert', split_axis=0, concat_...  36.7 us
    scatter-add x1, other arithmetic, memory_path(): dense = jnp.zeros((lookups * SHARD, width), jnp.float32).at[got_keys.resh...  11.7 us
    all_to_all x1, starting transfers between devices, memory_path(): lax.all_to_all(send_keys.reshape(groups, capacity), 'dp', split_axis=0, c...  11.1 us
    all_to_all x1, starting transfers between devices, per_device(): lax.all_to_all(expert_grad, 'expert', split_axis=0, concat_axis=0, tiled=...  8.64 us
    dot_general x1, matrix products, per_device(): jnp.einsum('sech,edh->secd', slope, lax.all_gather(up_weight, 'dp', axis=...  8.16 us
    all_to_all x1, starting transfers between devices, per_device(): lax.all_to_all(send_input.reshape(shape), 'expert', split_axis=0, concat_...  6.49 us
  transfers between devices with their start and end apart: 8, of which 4 were waited for; matrix products, arithmetic and copies ran while one was open for 23% of the time, Pallas kernels for 0%

commit v1 on v0

v1 whole, which is shorter than its diff:
```python
import functools

import jax
import jax.numpy as jnp
from jax import lax
from jax.experimental import pallas as pl
from jax.experimental.pallas import tpu as pltpu
from jax.sharding import PartitionSpec as P

MESH = pl.DeviceIdType.MESH
F32 = jnp.float32
BF16 = jnp.bfloat16
NZ = 8
XL = 2
CORES = 2
NE = 8
EXPERTS = NE * CORES
TOK = 128
D = 2560
HID = 512
CAP = 32
HALF = D // 2
Q = 2
QW = HALF // Q
UPR = D // (XL * NZ * CORES)
DNR = HID // (XL * NZ * CORES)
BLOCKS = NZ * CORES
GROUP = XL * CORES * NE
TROWS = GROUP * 2 * 16


def mod(value, size):
    return lax.rem(value + size, size)


def nt_dot(a, b):
    return lax.dot_general(a, b, (((1,), (1,)), ((), ())), preferred_element_type=F32)


def kernel(
    grad_ref, input_ref, up_ref, down_ref, emeta_ref, mmeta_ref,
    gi_ref, table_ref,
    up_buf, down_buf, pick, blend, send_x, send_g, got_x, got_g, slope_buf, ret_send, ret_got,
    gbuf, mbuf, sel, dense, rs_got,
    pre_recv, pre_send, w_recv, w_send, m_recv, m_send, t_recv, t_send,
    d_recv, d_send, r_recv, r_send, rs_recv, rs_send,
):
    dp = lax.axis_index("dp")
    e = lax.axis_index("expert")
    c = lax.rem(dp, 2)
    z = lax.rem(dp // 2, NZ)
    xl = dp // (2 * NZ)
    oc = 1 - c
    oxl = 1 - xl

    def dp_of(xl_, z_, c_):
        return (xl_ * NZ + z_) * 2 + c_

    def dev(xl_, z_, c_, e_):
        return {"dp": dp_of(xl_, z_, c_), "expert": e_}

    sibling = dev(xl, z, oc, e)
    ring = (dev(xl, mod(z + 1, NZ), c, e), dev(xl, mod(z - 1, NZ), c, e))
    me16 = e * 2 + c
    me32 = (xl * 2 + c) * NE + e

    def peer16(m):
        return dev(xl, z, lax.rem(m, 2), m // 2)

    def peer32(m):
        return dev(m // (2 * NE), z, lax.rem(m // NE, 2), lax.rem(m, NE))

    def remote(src, dst, send, recv, device):
        return pltpu.make_async_remote_copy(
            src_ref=src, dst_ref=dst, send_sem=send, recv_sem=recv,
            device_id=device, device_id_type=MESH,
        )

    barrier = pltpu.get_barrier_semaphore()
    for d in range(2):
        pl.semaphore_signal(barrier, inc=1, device_id=ring[d], device_id_type=MESH)

    @pl.loop(1, GROUP)
    def _(k):
        pl.semaphore_signal(
            barrier, inc=1, device_id=peer32(lax.rem(me32 + k, GROUP)), device_id_type=MESH
        )

    def up_rows(dp_, count):
        return pl.ds(pl.multiple_of(dp_ * UPR, 16), count)

    def down_rows(dp_, count):
        return pl.ds(pl.multiple_of(dp_ * DNR, 16), count)

    def tok_rows(block):
        return pl.ds(pl.multiple_of(block * TOK, TOK), TOK)

    def half_cols(order, q):
        return pl.ds(pl.multiple_of(order * HALF + q * QW, 128), QW)

    up_buf[up_rows(dp, UPR), :] = up_ref[c]
    down_buf[down_rows(dp, DNR), :] = down_ref[c]
    mine = z * 2 + c
    mbuf[mine] = mmeta_ref[c]
    for q in range(Q):
        gbuf[q, tok_rows(mine), :] = grad_ref[:, half_cols(c, q)]

    pl.semaphore_wait(barrier, GROUP - 1 + 2)

    pre = []
    for at, (src_core, device) in enumerate(
        ((oc, sibling), (c, dev(oxl, z, c, e)), (oc, dev(oxl, z, oc, e)))
    ):
        pre.append(remote(
            up_ref.at[src_core], up_buf.at[up_rows(dp, UPR)],
            pre_send.at[2 * at], pre_recv.at[2 * at], device,
        ))
        pre.append(remote(
            down_ref.at[src_core], down_buf.at[down_rows(dp, DNR)],
            pre_send.at[2 * at + 1], pre_recv.at[2 * at + 1], device,
        ))
    pre.append(remote(mmeta_ref.at[oc], mbuf.at[mine], pre_send.at[6], pre_recv.at[6], sibling))
    for q in range(Q):
        pre.append(remote(
            grad_ref.at[:, half_cols(oc, q)], gbuf.at[q, tok_rows(mine)],
            pre_send.at[7 + q], pre_recv.at[7 + q], sibling,
        ))
    for copy in pre:
        copy.start()
    theirs = z * 2 + oc
    arrivals = []
    for dp_ in (dp_of(xl, z, oc), dp_of(oxl, z, c), dp_of(oxl, z, oc)):
        arrivals.append(up_buf.at[up_rows(dp_, UPR)])
        arrivals.append(down_buf.at[down_rows(dp_, DNR)])
    arrivals.append(mbuf.at[theirs])
    for q in range(Q):
        arrivals.append(gbuf.at[q, tok_rows(theirs)])

    def pre_wait(at):
        remote(arrivals[at], arrivals[at], pre_send.at[at], pre_recv.at[at], sibling).wait_recv()

    def origin(d, s):
        return mod(z - s, NZ) if d == 0 else mod(z + s, NZ)

    def ring_block(kind, d, zs):
        if kind == "up":
            return up_buf.at[up_rows(dp_of((xl, oxl)[d], zs, 0), 2 * UPR)]
        if kind == "down":
            return down_buf.at[down_rows(dp_of((xl, oxl)[d], zs, 0), 2 * DNR)]
        block = zs * 2 + (c, oc)[d]
        if kind == "meta":
            return mbuf.at[block]
        return gbuf.at[kind, tok_rows(block)]

    def ring_sems(kind, d, s):
        if kind == "up":
            return w_send.at[0], w_recv.at[d, 0, s]
        if kind == "down":
            return w_send.at[1], w_recv.at[d, 1, s]
        if kind == "meta":
            return m_send, m_recv.at[d, s]
        return t_send.at[kind], t_recv.at[d, kind, s]

    def ring_send(kind, d, s):
        block = ring_block(kind, d, origin(d, s))
        send, recv = ring_sems(kind, d, s)
        remote(block, block, send, recv, ring[d]).start()

    def ring_wait(kind, d, s):
        block = ring_block(kind, d, origin(d, s + 1))
        send, recv = ring_sems(kind, d, s)
        remote(block, block, send, recv, ring[d]).wait_recv()

    def ring_step(kinds, s):
        for kind in kinds:
            for d in range(2):
                ring_wait(kind, d, s - 1)
                if s < NZ - 1:
                    ring_send(kind, d, s)

    ids = (emeta_ref[0:1, :], emeta_ref[1:2, :])
    gates = (emeta_ref[2:3, :], emeta_ref[3:4, :])
    numbers = lax.broadcasted_iota(jnp.int32, (EXPERTS, TOK), 0).astype(F32)
    zeros = jnp.zeros((EXPERTS, TOK), F32)
    hit0, hit1 = numbers == ids[0], numbers == ids[1]
    hits = jnp.where(hit0 | hit1, 1.0, 0.0)
    weight = jnp.where(hit0, gates[0], zeros) + jnp.where(hit1, gates[1], zeros)
    earlier = jnp.where(
        lax.broadcasted_iota(jnp.int32, (TOK, TOK), 0)
        < lax.broadcasted_iota(jnp.int32, (TOK, TOK), 1),
        1.0, 0.0,
    ).astype(BF16)
    rank = jnp.dot(hits.astype(BF16), earlier, preferred_element_type=F32)
    place = jnp.where(hits > 0.5, rank, -1.0)
    slots = lax.broadcasted_iota(jnp.int32, (CAP, TOK), 0).astype(F32)
    for x in range(EXPERTS):
        chosen = slots == place[x : x + 1, :]
        pick[x * CAP : (x + 1) * CAP, :] = jnp.where(chosen, 1.0, 0.0).astype(BF16)
        blend[x * CAP : (x + 1) * CAP, :] = jnp.where(chosen, weight[x : x + 1, :], 0.0)

    pre_wait(0)
    ring_send("up", 0, 0)
    pre_wait(1)
    ring_send("down", 0, 0)
    pre_wait(6)
    for d in range(2):
        ring_send("meta", d, 0)

    own = me16 // 4

    def dispatch(i):
        first = lax.rem(own + i, 4) * 4
        rows = pl.ds(pl.multiple_of(first * CAP, 128), 4 * CAP)
        onehot = pick[rows, :]

        @pl.loop(0, 5)
        def _(n):
            cols = pl.ds(pl.multiple_of(n * 512, 512), 512)
            send_x[rows, cols] = jnp.dot(
                onehot, input_ref[:, cols], preferred_element_type=F32
            ).astype(BF16)
            send_g[rows, cols] = jnp.dot(
                onehot, grad_ref[:, cols], preferred_element_type=F32
            ).astype(BF16)

    def slot_rows(m):
        return pl.ds(pl.multiple_of(m * CAP, CAP), CAP)

    def dispatch_sends(i):
        @pl.loop(0, 4)
        def _(k):
            m = lax.rem(own + i, 4) * 4 + lax.rem(me16 + k, 4)

            @pl.when(m != me16)
            def _():
                remote(
                    send_x.at[slot_rows(m)], got_x.at[slot_rows(me16)],
                    d_send.at[0], d_recv.at[0], peer16(m),
                ).start()
                remote(
                    send_g.at[slot_rows(m)], got_g.at[slot_rows(me16)],
                    d_send.at[1], d_recv.at[1], peer16(m),
                ).start()

    dispatch(1)
    dispatch_sends(1)
    pre_wait(2)
    pre_wait(4)
    ring_send("up", 1, 0)
    pre_wait(3)
    pre_wait(5)
    ring_send("down", 1, 0)
    for i in (2, 3, 0):
        dispatch(i)
        dispatch_sends(i)
    got_x[slot_rows(me16), :] = send_x[slot_rows(me16), :]
    got_g[slot_rows(me16), :] = send_g[slot_rows(me16), :]

    for s in range(1, 4):
        ring_step(("up", "down", "meta"), s)
    pre_wait(7)
    for s in range(4, 8):
        ring_step(("up", "down", "meta"), s)
        if s == 4:
            for d in range(2):
                ring_send(0, d, 0)
        else:
            ring_step((0,), s - 4)

    def all_bytes(ref, sem):
        pltpu.make_async_copy(ref, ref, sem).wait()

    some = pl.ds(0, (EXPERTS - 1) * CAP)
    all_bytes(got_x.at[some], d_recv.at[0])
    all_bytes(got_g.at[some], d_recv.at[1])

    def expert(i):
        rows = pl.ds(i * 256, 256)

        @pl.loop(0, 2)
        def _(n):
            cols = pl.ds(pl.multiple_of(n * 256, 256), 256)
            before = jnp.dot(got_x[rows, :], up_buf[:, cols], preferred_element_type=F32)
            back = nt_dot(got_g[rows, :], down_buf[cols, :])
            sig = 1.0 / (1.0 + jnp.exp(-before))
            slope_buf[:, cols] = (back * sig * (1.0 + before * (1.0 - sig))).astype(BF16)

        @pl.loop(0, D // 256)
        def _(n):
            cols = pl.ds(pl.multiple_of(n * 256, 256), 256)
            ret_send[rows, cols] = nt_dot(slope_buf[...], up_buf[cols, :]).astype(BF16)

        @pl.loop(0, 8)
        def _(k):
            m = i * 8 + lax.rem(me16 + k, 8)

            @pl.when(m != me16)
            def _():
                remote(
                    ret_send.at[slot_rows(m)], ret_got.at[slot_rows(me16)],
                    r_send, r_recv, peer16(m),
                ).start()

    pre_wait(8)
    expert(0)
    ring_step((0,), 4)
    for d in range(2):
        ring_send(1, d, 0)
    expert(1)
    ret_got[slot_rows(me16), :] = ret_send[slot_rows(me16), :]
    ring_step((0, ), 5)
    ring_step((1, ), 1)

    targets = (lax.broadcasted_iota(jnp.int32, (TROWS, TOK), 0) + z * TROWS).astype(F32)

    def select(block):
        cols = pl.ds(pl.multiple_of(block * TOK, TOK), TOK)
        meta = mbuf[block]
        one = jnp.where(targets == meta[1:2, :], meta[3:4, :], 0.0)
        sel[:, cols] = jnp.where(targets == meta[0:1, :], meta[2:3, :], one).astype(BF16)

    pl.loop(0, BLOCKS // 2)(select)
    ring_step((0, ), 6)
    ring_step((1, ), 2)
    pl.loop(BLOCKS // 2, BLOCKS)(select)
    ring_step((0, ), 7)
    ring_step((1, ), 3)

    def table_rows(m):
        return pl.ds(pl.multiple_of(m * 32, 32), 32)

    def table_part(q):
        @pl.loop(0, TROWS // 256)
        def _(i):
            rows = pl.ds(pl.multiple_of(i * 256, 256), 256)
            dense[q, rows, :] = jnp.dot(
                sel[rows, :], gbuf[q], preferred_element_type=F32
            ).astype(BF16)

        @pl.loop(1, GROUP)
        def _(k):
            m = lax.rem(me32 + k, GROUP)
            remote(
                dense.at[q, table_rows(m)], rs_got.at[q, (c * 2 + xl) * NE + e],
                rs_send.at[q], rs_recv.at[q], peer32(m),
            ).start()

        rs_got[q, (c * 2 + xl) * NE + e] = dense[q, table_rows(me32), :]

    def table_sum(q):
        all_bytes(rs_got.at[q, pl.ds(0, GROUP - 1)], rs_recv.at[q])
        for order in range(2):
            total = rs_got[q, order * 16].astype(F32)
            for k in range(1, 16):
                total += rs_got[q, order * 16 + k].astype(F32)
            table_ref[order * 2 : order * 2 + 2, :, q * QW : (q + 1) * QW] = total.reshape(
                2, 16, QW
            )

    table_part(0)
    for s in range(4, 7):
        ring_step((1, ), s)

    all_bytes(ret_got.at[some], r_recv)
    mix = blend[...].T.astype(BF16)

    @pl.loop(0, D // 256)
    def _(n):
        cols = pl.ds(pl.multiple_of(n * 256, 256), 256)
        gi_ref[:, cols] = jnp.dot(mix, ret_got[:, cols], preferred_element_type=F32).astype(BF16)

    ring_step((1, ), 7)
    table_part(1)
    table_sum(0)
    table_sum(1)

    for copy in pre:
        copy.wait_send()
    sends = 2 * (NZ - 1)
    all_bytes(up_buf.at[pl.ds(0, sends * 2 * UPR)], w_send.at[0])
    all_bytes(down_buf.at[pl.ds(0, sends * 2 * DNR)], w_send.at[1])
    all_bytes(mbuf.at[pl.ds(0, sends)], m_send)
    for q in range(Q):
        all_bytes(gbuf.at[q, pl.ds(0, sends * TOK)], t_send.at[q])
        all_bytes(dense.at[q, pl.ds(0, (GROUP - 1) * 32)], rs_send.at[q])
    all_bytes(send_x.at[some], d_send.at[0])
    all_bytes(send_g.at[some], d_send.at[1])
    all_bytes(ret_send.at[some], r_send)


def per_device(
    grad_out, saved_input, expert_ids, gate_weights, up_weight, down_weight,
    engram_gate, memory_owner, memory_slot,
):
    emeta = jnp.concatenate(
        [expert_ids.astype(F32).T, gate_weights.T, jnp.zeros((4, TOK), F32)], axis=0
    )
    head = jnp.arange(4, dtype=jnp.int32)[None, :] % 2
    core = memory_owner % 2
    zs = (memory_owner // 2) % NZ
    xs = memory_owner // (2 * NZ)
    row = (((zs * XL + xs) * 2 + core) * NE + memory_slot // 16) * 32
    row = row + head * 16 + memory_slot % 16
    rows_t = row.astype(F32).T.reshape(2, 2, TOK)
    gates_t = engram_gate.T.reshape(2, 2, TOK)
    mmeta = jnp.concatenate([rows_t, gates_t, jnp.zeros((2, 4, TOK), F32)], axis=1)

    vmem = pl.BlockSpec(memory_space=pltpu.VMEM)
    dma = pltpu.SemaphoreType.DMA
    return pl.pallas_call(
        kernel,
        out_shape=(
            jax.ShapeDtypeStruct((TOK, D), BF16),
            jax.ShapeDtypeStruct((4, 16, HALF), F32),
        ),
        in_specs=[vmem] * 6,
        out_specs=(vmem, vmem),
        scratch_shapes=[
            pltpu.VMEM((D, HID), BF16),
            pltpu.VMEM((HID, D), BF16),
            pltpu.VMEM((EXPERTS * CAP, TOK), BF16),
            pltpu.VMEM((EXPERTS * CAP, TOK), F32),
            pltpu.VMEM((EXPERTS * CAP, D), BF16),
            pltpu.VMEM((EXPERTS * CAP, D), BF16),
            pltpu.VMEM((EXPERTS * CAP, D), BF16),
            pltpu.VMEM((EXPERTS * CAP, D), BF16),
            pltpu.VMEM((256, HID), BF16),
            pltpu.VMEM((EXPERTS * CAP, D), BF16),
            pltpu.VMEM((EXPERTS * CAP, D), BF16),
            pltpu.VMEM((Q, BLOCKS * TOK, QW), BF16),
            pltpu.VMEM((BLOCKS, 8, TOK), F32),
            pltpu.VMEM((TROWS, BLOCKS * TOK), BF16),
            pltpu.VMEM((Q, TROWS, QW), BF16),
            pltpu.VMEM((Q, GROUP, 32, QW), BF16),
            dma((7 + Q,)),
            dma((7 + Q,)),
            dma((2, 2, NZ - 1)),
            dma((2,)),
            dma((2, NZ - 1)),
            dma(()),
            dma((2, Q, NZ - 1)),
            dma((Q,)),
            dma((2,)),
            dma((2,)),
            dma(()),
            dma(()),
            dma((Q,)),
            dma((Q,)),
        ],
        compiler_params=pltpu.CompilerParams(
            collective_id=0, has_side_effects=True, vmem_limit_bytes=58 * 1024 * 1024
        ),
        cost_estimate=pl.CostEstimate(
            flops=10_000_000_000, bytes_accessed=4_000_000, transcendentals=262_144
        ),
    )(grad_out, saved_input, up_weight, down_weight, emeta, mmeta)


def solution(mesh):
    tokens = P(("dp", "expert"), None)
    return jax.shard_map(
        per_device,
        mesh=mesh,
        in_specs=(
            tokens, tokens, tokens, tokens,
            P("expert", "dp", None), P("expert", "dp", None),
            tokens, tokens, tokens,
        ),
        out_specs=(tokens, P(None, ("dp", "expert"), None)),
        check_vma=False,
    )
```

time: 319 us -> 164 us (0.51)
  waiting for transfers between devices: 182 us -> 0 us
  Pallas kernels: 0 us -> 157 us
  starting transfers between devices: 36.3 us -> 0 us
  local copies, waits for them, and re-layouts: 38.7 us -> 4.2 us
  other arithmetic: 30.4 us -> 1.41 us
  between operations: 15.7 us -> 0.68 us
  matrix products: 13.9 us -> 0 us
    pallas_call x0 -> x1, Pallas kernels: none -> 157 us  [per_device(): pl.pallas_call(kernel, out_shape=(jax.ShapeDtypeStruct((TOK, D), BF16), j...]
    all_to_all x5 -> x0, waiting for transfers between devices: 111 us -> none  [the longest x1 68.6 us: memory_path(): lax.all_to_all(send_rows.reshape(groups, capacity, width), 'dp', split_ax...]
    reduce_scatter x1 -> x0, waiting for transfers between devices: 69.5 us -> none  [memory_path(): lax.psum_scatter(dense.reshape(lookups, SHARD, width).astype(jnp.bfloat16...]
    all_to_all x5 -> x0, starting transfers between devices: 36.2 us -> none  [the longest x1 11.1 us: memory_path(): lax.all_to_all(send_keys.reshape(groups, capacity), 'dp', split_axis=0, c...]
    dot_general x2 -> x0, matrix products: 13.9 us -> none  [the longest x1 8.16 us: per_device(): jnp.einsum('sech,edh->secd', slope, lax.all_gather(up_weight, 'dp', axis=...]
    scatter x3 -> x0, local copies, waits for them, and re-layouts: 11.8 us -> none  [the longest x1 5.07 us: per_device(): send_grad = jnp.zeros((experts * capacity, width), jnp.bfloat16).at[place...]
    scatter-add x1 -> x0, other arithmetic: 11.7 us -> none  [memory_path(): dense = jnp.zeros((lookups * SHARD, width), jnp.float32).at[got_keys.resh...]
    convert_element_type x4 -> x0, local copies, waits for them, and re-layouts: 9.04 us -> none  [the longest x2 4.25 us: memory_path(): jnp.repeat(halves, HEADS, axis=1).astype(jnp.float32)]
  transfers between devices with their start and end apart: 8 -> 0, of which waited for: 4 -> 0; matrix products, arithmetic and copies ran while one was open for 23% -> 0% of each run, Pallas kernels for 0% -> 0%
where the time goes in v1:
time: 164 us
  Pallas kernels  157 us (96%)
  local copies, waits for them, and re-layouts  4.2 us (3%)
    pallas_call x1, Pallas kernels, per_device(): pl.pallas_call(kernel, out_shape=(jax.ShapeDtypeStruct((TOK, D), BF16), j...  157 us
    unnamed x14, local copies, waits for them, and re-layouts  4.12 us

profile of v1, /device:TPU:1, one launch (start us, length us, event | category | flops | bytes accessed | tf_op | source)
XLA Modules:
  0.0 163.7 jit_solution(16472035901405902051)
XLA Ops:
  0.6 0.0 copy-start.4
  0.7 0.0 copy-start.3
  0.7 0.1 pad.5.clone
  0.7 0.0 copy-start.2
  0.7 0.6 copy-done.4
  1.3 0.0 copy-done.3
  1.3 0.1 copy-done.2
  1.4 0.1 fusion.10
  1.5 0.0 copy-start.5
  1.5 0.7 copy-done.5
  2.2 0.0 copy-start.1
  2.2 0.7 maximum_maximum_fusion.1.emeta_ref
  2.8 0.0 copy-done.1
  2.9 0.7 maximum_maximum_fusion.mmeta_ref
  3.5 157.4 %shard_map.104 = (bf16[128,2560]{1,0:T(8,128)(2,1)}, f32[4,16,1280]{2,1,0:T(8,128)}) custom-call(bf16[128,2560]{1,0:T(8,128)(2,1)} %grad_ref.1, bf16[128,2560]{1,0:T(8,128)(2,1)} %input_ref.1, bf16[2,80,512]{2,1,0:T(8,128)(2,1)} %up_ref.1, bf16[2,16,2560]{2,1,0:T(8,128)(2,1)} %down_ref.1, f32[8,128]{1,0:T(8,128)} %maximum_maximum_fusion.1.emeta_ref, ...), custom_call_target="tpu_custom_call" | custom-call | flops 10000000000 | bytes 4000000 | tf_op jit(solution)/shard_map/pallas_call | solution.py:410
  160.9 0.0 copy-start
  160.9 2.0 %copy.13 = bf16[128,2560]{1,0:T(8,128)(2,1)} copy(bf16[128,2560]{1,0:T(8,128)(2,1)} %get-tuple-element.4) | data formatting | bytes 1310720
  163.0 0.0 copy-done
  163.0 0.7 copy.14
  (3 shorter events, 0.0 us)
Async XLA Ops:
  0.6 0.7 copy-start.4
  0.7 0.7 copy-start.3
  0.7 0.7 copy-start.2
  1.5 0.7 copy-start.5
  2.2 0.7 copy-start.1
  160.9 2.0 %copy-start = (f32[4,16,1280]{2,1,0:T(8,128)S(1)}, f32[4,16,1280]{2,1,0:T(8,128)}, u32[]{:S(2)}) copy-start(f32[4,16,1280]{2,1,0:T(8,128)} %get-tuple-element.5) | copy-start | bytes 983044

commit v2 on v1

--- a/solution.py
+++ b/solution.py
@@ -20,7 +20,7 @@
 HID = 512
 CAP = 32
 HALF = D // 2
-Q = 2
+Q = 5
 QW = HALF // Q
 UPR = D // (XL * NZ * CORES)
 DNR = HID // (XL * NZ * CORES)
@@ -42,7 +42,7 @@
     gi_ref, table_ref,
     up_buf, down_buf, pick, blend, send_x, send_g, got_x, got_g, slope_buf, ret_send, ret_got,
     gbuf, mbuf, sel, dense, rs_got,
-    pre_recv, pre_send, w_recv, w_send, m_recv, m_send, t_recv, t_send,
+    pre_recv, pre_send, w_recv, w_send, x_recv, x_send, m_recv, m_send, t_recv, t_send,
     d_recv, d_send, r_recv, r_send, rs_recv, rs_send,
 ):
     dp = lax.axis_index("dp")
@@ -65,7 +65,9 @@
     me32 = (xl * 2 + c) * NE + e
 
     def peer16(m):
-        return dev(xl, z, lax.rem(m, 2), m // 2)
+        e_ = m // 2
+        xl_ = jnp.where(e_ // (NE // 2) == e // (NE // 2), xl, oxl)
+        return dev(xl_, z, lax.rem(m, 2), e_)
 
     def peer32(m):
         return dev(m // (2 * NE), z, lax.rem(m // NE, 2), lax.rem(m, NE))
@@ -100,83 +102,10 @@
 
     up_buf[up_rows(dp, UPR), :] = up_ref[c]
     down_buf[down_rows(dp, DNR), :] = down_ref[c]
-    mine = z * 2 + c
+    mine, theirs = z * 2 + c, z * 2 + oc
     mbuf[mine] = mmeta_ref[c]
     for q in range(Q):
         gbuf[q, tok_rows(mine), :] = grad_ref[:, half_cols(c, q)]
-
-    pl.semaphore_wait(barrier, GROUP - 1 + 2)
-
-    pre = []
-    for at, (src_core, device) in enumerate(
-        ((oc, sibling), (c, dev(oxl, z, c, e)), (oc, dev(oxl, z, oc, e)))
-    ):
-        pre.append(remote(
-            up_ref.at[src_core], up_buf.at[up_rows(dp, UPR)],
-            pre_send.at[2 * at], pre_recv.at[2 * at], device,
-        ))
-        pre.append(remote(
-            down_ref.at[src_core], down_buf.at[down_rows(dp, DNR)],
-            pre_send.at[2 * at + 1], pre_recv.at[2 * at + 1], device,
-        ))
-    pre.append(remote(mmeta_ref.at[oc], mbuf.at[mine], pre_send.at[6], pre_recv.at[6], sibling))
-    for q in range(Q):
-        pre.append(remote(
-            grad_ref.at[:, half_cols(oc, q)], gbuf.at[q, tok_rows(mine)],
-            pre_send.at[7 + q], pre_recv.at[7 + q], sibling,
-        ))
-    for copy in pre:
-        copy.start()
-    theirs = z * 2 + oc
-    arrivals = []
-    for dp_ in (dp_of(xl, z, oc), dp_of(oxl, z, c), dp_of(oxl, z, oc)):
-        arrivals.append(up_buf.at[up_rows(dp_, UPR)])
-        arrivals.append(down_buf.at[down_rows(dp_, DNR)])
-    arrivals.append(mbuf.at[theirs])
-    for q in range(Q):
-        arrivals.append(gbuf.at[q, tok_rows(theirs)])
-
-    def pre_wait(at):
-        remote(arrivals[at], arrivals[at], pre_send.at[at], pre_recv.at[at], sibling).wait_recv()
-
-    def origin(d, s):
-        return mod(z - s, NZ) if d == 0 else mod(z + s, NZ)
-
-    def ring_block(kind, d, zs):
-        if kind == "up":
-            return up_buf.at[up_rows(dp_of((xl, oxl)[d], zs, 0), 2 * UPR)]
-        if kind == "down":
-            return down_buf.at[down_rows(dp_of((xl, oxl)[d], zs, 0), 2 * DNR)]
-        block = zs * 2 + (c, oc)[d]
-        if kind == "meta":
-            return mbuf.at[block]
-        return gbuf.at[kind, tok_rows(block)]
-
-    def ring_sems(kind, d, s):
-        if kind == "up":
-            return w_send.at[0], w_recv.at[d, 0, s]
-        if kind == "down":
-            return w_send.at[1], w_recv.at[d, 1, s]
-        if kind == "meta":
-            return m_send, m_recv.at[d, s]
-        return t_send.at[kind], t_recv.at[d, kind, s]
-
-    def ring_send(kind, d, s):
-        block = ring_block(kind, d, origin(d, s))
-        send, recv = ring_sems(kind, d, s)
-        remote(block, block, send, recv, ring[d]).start()
-
-    def ring_wait(kind, d, s):
-        block = ring_block(kind, d, origin(d, s + 1))
-        send, recv = ring_sems(kind, d, s)
-        remote(block, block, send, recv, ring[d]).wait_recv()
-
-    def ring_step(kinds, s):
-        for kind in kinds:
-            for d in range(2):
-                ring_wait(kind, d, s - 1)
-                if s < NZ - 1:
-                    ring_send(kind, d, s)
 
     ids = (emeta_ref[0:1, :], emeta_ref[1:2, :])
     gates = (emeta_ref[2:3, :], emeta_ref[3:4, :])
@@ -198,14 +127,6 @@
         pick[x * CAP : (x + 1) * CAP, :] = jnp.where(chosen, 1.0, 0.0).astype(BF16)
         blend[x * CAP : (x + 1) * CAP, :] = jnp.where(chosen, weight[x : x + 1, :], 0.0)
 
-    pre_wait(0)
-    ring_send("up", 0, 0)
-    pre_wait(1)
-    ring_send("down", 0, 0)
-    pre_wait(6)
-    for d in range(2):
-        ring_send("meta", d, 0)
-
     own = me16 // 4
 
     def dispatch(i):
@@ -243,36 +164,125 @@
                 ).start()
 
     dispatch(1)
+    pl.semaphore_wait(barrier, GROUP - 1 + 2)
+
+    pre = [
+        remote(up_ref.at[oc], up_buf.at[up_rows(dp, UPR)], pre_send.at[0], pre_recv.at[0], sibling),
+        remote(
+            down_ref.at[oc], down_buf.at[down_rows(dp, DNR)],
+            pre_send.at[1], pre_recv.at[1], sibling,
+        ),
+        remote(mmeta_ref.at[oc], mbuf.at[mine], pre_send.at[2], pre_recv.at[2], sibling),
+    ]
+    for q in range(Q):
+        pre.append(remote(
+            grad_ref.at[:, half_cols(oc, q)], gbuf.at[q, tok_rows(mine)],
+            pre_send.at[3 + q], pre_recv.at[3 + q], sibling,
+        ))
+    arrivals = [
+        up_buf.at[up_rows(dp_of(xl, z, oc), UPR)],
+        down_buf.at[down_rows(dp_of(xl, z, oc), DNR)],
+        mbuf.at[theirs],
+    ]
+    for q in range(Q):
+        arrivals.append(gbuf.at[q, tok_rows(theirs)])
+
+    def pre_wait(at):
+        remote(arrivals[at], arrivals[at], pre_send.at[at], pre_recv.at[at], sibling).wait_recv()
+
+    def origin(d, s):
+        return mod(z - s, NZ) if d == 0 else mod(z + s, NZ)
+
+    def ring_block(kind, d, zs):
+        if kind == "weights":
+            if d == 0:
+                return up_buf.at[up_rows(dp_of(xl, zs, 0), 2 * UPR)]
+            return down_buf.at[down_rows(dp_of(xl, zs, 0), 2 * DNR)]
+        block = zs * 2 + (c, oc)[d]
+        if kind == "meta":
+            return mbuf.at[block]
+        return gbuf.at[kind, tok_rows(block)]
+
+    def ring_sems(kind, d, s):
+        if kind == "weights":
+            return w_send.at[d], w_recv.at[d, s]
+        if kind == "meta":
+            return m_send, m_recv.at[d, s]
+        return t_send.at[kind], t_recv.at[d, kind, s]
+
+    def ring_send(kind, d, s):
+        block = ring_block(kind, d, origin(d, s))
+        send, recv = ring_sems(kind, d, s)
+        remote(block, block, send, recv, ring[d]).start()
+
+    def ring_wait(kind, d, s):
+        block = ring_block(kind, d, origin(d, s + 1))
+        send, recv = ring_sems(kind, d, s)
+        remote(block, block, send, recv, ring[d]).wait_recv()
+
+    across = dev(oxl, z, c, e)
+
+    def cross(d, zs):
+        block = ring_block("weights", d, zs)
+        remote(block, block, x_send.at[d], x_recv.at[d], across).start()
+
+    def ring_step(kinds, s):
+        for kind in kinds:
+            for d in range(2):
+                ring_wait(kind, d, s - 1)
+                if s < NZ - 1:
+                    ring_send(kind, d, s)
+                if kind == "weights":
+                    cross(d, origin(d, s))
+
+    remote(
+        up_ref.at[c], up_buf.at[up_rows(dp, UPR)], w_send.at[0], w_recv.at[0, 0], ring[0]
+    ).start()
+    remote(
+        down_ref.at[c], down_buf.at[down_rows(dp, DNR)], w_send.at[1], w_recv.at[1, 0], ring[1]
+    ).start()
+    for copy in pre[:5]:
+        copy.start()
+    ring_send(0, 0, 0)
+    ring_send(1, 0, 0)
     dispatch_sends(1)
+    dispatch(2)
+    pre_wait(0)
+    remote(
+        arrivals[0], arrivals[0], w_send.at[0], w_recv.at[0, 0], ring[0]
+    ).start()
+    cross(0, z)
+    pre_wait(1)
+    remote(
+        arrivals[1], arrivals[1], w_send.at[1], w_recv.at[1, 0], ring[1]
+    ).start()
+    cross(1, z)
     pre_wait(2)
-    pre_wait(4)
-    ring_send("up", 1, 0)
-    pre_wait(3)
-    pre_wait(5)
-    ring_send("down", 1, 0)
-    for i in (2, 3, 0):
+    for d in range(2):
+        ring_send("meta", d, 0)
+    for q in range(2):
+        pre_wait(3 + q)
+        ring_send(q, 1, 0)
+    dispatch_sends(2)
+    for copy in pre[5:]:
+        copy.start()
+    for i in (3, 0):
         dispatch(i)
         dispatch_sends(i)
     got_x[slot_rows(me16), :] = send_x[slot_rows(me16), :]
     got_g[slot_rows(me16), :] = send_g[slot_rows(me16), :]
 
-    for s in range(1, 4):
-        ring_step(("up", "down", "meta"), s)
-    pre_wait(7)
-    for s in range(4, 8):
-        ring_step(("up", "down", "meta"), s)
-        if s == 4:
-            for d in range(2):
-                ring_send(0, d, 0)
-        else:
-            ring_step((0,), s - 4)
+    for s in range(1, NZ):
+        ring_step(("weights", 0, 1, "meta"), s)
+    for q in range(2, Q):
+        pre_wait(3 + q)
+        for d in range(2):
+            ring_send(q, d, 0)
 
     def all_bytes(ref, sem):
         pltpu.make_async_copy(ref, ref, sem).wait()
 
     some = pl.ds(0, (EXPERTS - 1) * CAP)
-    all_bytes(got_x.at[some], d_recv.at[0])
-    all_bytes(got_g.at[some], d_recv.at[1])
 
     def expert(i):
         rows = pl.ds(i * 256, 256)
@@ -301,16 +311,6 @@
                     r_send, r_recv, peer16(m),
                 ).start()
 
-    pre_wait(8)
-    expert(0)
-    ring_step((0,), 4)
-    for d in range(2):
-        ring_send(1, d, 0)
-    expert(1)
-    ret_got[slot_rows(me16), :] = ret_send[slot_rows(me16), :]
-    ring_step((0, ), 5)
-    ring_step((1, ), 1)
-
     targets = (lax.broadcasted_iota(jnp.int32, (TROWS, TOK), 0) + z * TROWS).astype(F32)
 
     def select(block):
@@ -318,13 +318,6 @@
         meta = mbuf[block]
         one = jnp.where(targets == meta[1:2, :], meta[3:4, :], 0.0)
         sel[:, cols] = jnp.where(targets == meta[0:1, :], meta[2:3, :], one).astype(BF16)
-
-    pl.loop(0, BLOCKS // 2)(select)
-    ring_step((0, ), 6)
-    ring_step((1, ), 2)
-    pl.loop(BLOCKS // 2, BLOCKS)(select)
-    ring_step((0, ), 7)
-    ring_step((1, ), 3)
 
     def table_rows(m):
         return pl.ds(pl.multiple_of(m * 32, 32), 32)
@@ -357,9 +350,26 @@
                 2, 16, QW
             )
 
+    last = tuple(range(2, Q))
+    pl.loop(0, BLOCKS // 2)(select)
+    ring_step(last, 1)
+    pl.loop(BLOCKS // 2, BLOCKS)(select)
+    ring_step(last, 2)
     table_part(0)
-    for s in range(4, 7):
-        ring_step((1, ), s)
+    table_part(1)
+    ring_step(last, 3)
+    all_bytes(up_buf.at[up_rows(dp_of(oxl, 0, 0), NZ * 2 * UPR)], x_recv.at[0])
+    all_bytes(down_buf.at[down_rows(dp_of(oxl, 0, 0), NZ * 2 * DNR)], x_recv.at[1])
+    all_bytes(got_x.at[some], d_recv.at[0])
+    all_bytes(got_g.at[some], d_recv.at[1])
+    expert(0)
+    ring_step(last, 4)
+    expert(1)
+    ret_got[slot_rows(me16), :] = ret_send[slot_rows(me16), :]
+    for s in range(5, NZ):
+        ring_step(last, s)
+    for q in last:
+        table_part(q)
 
     all_bytes(ret_got.at[some], r_recv)
     mix = blend[...].T.astype(BF16)
@@ -369,16 +379,16 @@
         cols = pl.ds(pl.multiple_of(n * 256, 256), 256)
         gi_ref[:, cols] = jnp.dot(mix, ret_got[:, cols], preferred_element_type=F32).astype(BF16)
 
-    ring_step((1, ), 7)
-    table_part(1)
-    table_sum(0)
-    table_sum(1)
+    for q in range(Q):
+        table_sum(q)
 
     for copy in pre:
         copy.wait_send()
     sends = 2 * (NZ - 1)
-    all_bytes(up_buf.at[pl.ds(0, sends * 2 * UPR)], w_send.at[0])
-    all_bytes(down_buf.at[pl.ds(0, sends * 2 * DNR)], w_send.at[1])
+    all_bytes(up_buf.at[pl.ds(0, (NZ - 1) * 2 * UPR)], w_send.at[0])
+    all_bytes(down_buf.at[pl.ds(0, (NZ - 1) * 2 * DNR)], w_send.at[1])
+    all_bytes(up_buf.at[pl.ds(0, NZ * 2 * UPR)], x_send.at[0])
+    all_bytes(down_buf.at[pl.ds(0, NZ * 2 * DNR)], x_send.at[1])
     all_bytes(mbuf.at[pl.ds(0, sends)], m_send)
     for q in range(Q):
         all_bytes(gbuf.at[q, pl.ds(0, sends * TOK)], t_send.at[q])
@@ -432,9 +442,11 @@
             pltpu.VMEM((TROWS, BLOCKS * TOK), BF16),
             pltpu.VMEM((Q, TROWS, QW), BF16),
             pltpu.VMEM((Q, GROUP, 32, QW), BF16),
-            dma((7 + Q,)),
-            dma((7 + Q,)),
-            dma((2, 2, NZ - 1)),
+            dma((3 + Q,)),
+            dma((3 + Q,)),
+            dma((2, NZ - 1)),
+            dma((2,)),
+            dma((2,)),
             dma((2,)),
             dma((2, NZ - 1)),
             dma(()),

time: 164 us -> 149 us (0.909)
  Pallas kernels: 157 us -> 143 us
    pallas_call x1, Pallas kernels: 157 us -> 143 us  [per_device(): pl.pallas_call(kernel, out_shape=(jax.ShapeDtypeStruct((TOK, D), BF16), j...]
where the time goes in v2:
time: 149 us
  Pallas kernels  143 us (96%)
  local copies, waits for them, and re-layouts  4.2 us (3%)
    pallas_call x1, Pallas kernels, per_device(): pl.pallas_call(kernel, out_shape=(jax.ShapeDtypeStruct((TOK, D), BF16), j...  143 us
    unnamed x14, local copies, waits for them, and re-layouts  4.12 us

profile of v2, /device:TPU:1, one launch (start us, length us, event | category | flops | bytes accessed | tf_op | source)
XLA Modules:
  0.0 149.1 jit_solution(15773226794763753899)
XLA Ops:
  0.6 0.0 copy-start.4
  0.7 0.0 copy-start.3
  0.7 0.1 pad.5.clone
  0.7 0.0 copy-start.2
  0.7 0.6 copy-done.4
  1.3 0.0 copy-done.3
  1.3 0.1 copy-done.2
  1.4 0.1 fusion.10
  1.5 0.0 copy-start.5
  1.5 0.7 copy-done.5
  2.2 0.0 copy-start.1
  2.2 0.7 maximum_maximum_fusion.1.emeta_ref
  2.8 0.0 copy-done.1
  2.9 0.7 maximum_maximum_fusion.mmeta_ref
  3.5 142.9 %shard_map.104 = (bf16[128,2560]{1,0:T(8,128)(2,1)}, f32[4,16,1280]{2,1,0:T(8,128)}) custom-call(bf16[128,2560]{1,0:T(8,128)(2,1)} %grad_ref.1, bf16[128,2560]{1,0:T(8,128)(2,1)} %input_ref.1, bf16[2,80,512]{2,1,0:T(8,128)(2,1)} %up_ref.1, bf16[2,16,2560]{2,1,0:T(8,128)(2,1)} %down_ref.1, f32[8,128]{1,0:T(8,128)} %maximum_maximum_fusion.1.emeta_ref, ...), custom_call_target="tpu_custom_call" | custom-call | flops 10000000000 | bytes 4000000 | tf_op jit(solution)/shard_map/pallas_call | solution.py:420
  146.4 0.0 copy-start
  146.4 2.0 %copy.13 = bf16[128,2560]{1,0:T(8,128)(2,1)} copy(bf16[128,2560]{1,0:T(8,128)(2,1)} %get-tuple-element.4) | data formatting | bytes 1310720
  148.4 0.0 copy-done
  148.4 0.7 copy.14
  (3 shorter events, 0.0 us)
Async XLA Ops:
  0.6 0.7 copy-start.4
  0.7 0.7 copy-start.3
  0.7 0.7 copy-start.2
  1.5 0.7 copy-start.5
  2.2 0.7 copy-start.1
  146.4 2.0 %copy-start = (f32[4,16,1280]{2,1,0:T(8,128)S(1)}, f32[4,16,1280]{2,1,0:T(8,128)}, u32[]{:S(2)}) copy-start(f32[4,16,1280]{2,1,0:T(8,128)} %get-tuple-element.5) | copy-start | bytes 983044

commit v3 on v2

--- a/solution.py
+++ b/solution.py
@@ -13,7 +13,11 @@
 NZ = 8
 XL = 2
 CORES = 2
-NE = 8
+XH = 2
+NY = 4
+NE = XH * NY
+NX = XH * XL
+PEERS = NY * CORES
 EXPERTS = NE * CORES
 TOK = 128
 D = 2560
@@ -25,8 +29,9 @@
 UPR = D // (XL * NZ * CORES)
 DNR = HID // (XL * NZ * CORES)
 BLOCKS = NZ * CORES
-GROUP = XL * CORES * NE
-TROWS = GROUP * 2 * 16
+XROWS = PEERS * 2 * 16
+TROWS = NX * XROWS
+SET = PEERS * CAP
 
 
 def mod(value, size):
@@ -40,37 +45,38 @@
 def kernel(
     grad_ref, input_ref, up_ref, down_ref, emeta_ref, mmeta_ref,
     gi_ref, table_ref,
-    up_buf, down_buf, pick, blend, send_x, send_g, got_x, got_g, slope_buf, ret_send, ret_got,
-    gbuf, mbuf, sel, dense, rs_got,
+    up_buf, down_buf, far_x, far_g, far_meta, pick, far_pick, blend,
+    send_x, send_g, got_x, got_g, slope_buf, ret_send, ret_got,
+    gbuf, mbuf, sel, dense, s1_got, s2_send, s2_got,
     pre_recv, pre_send, w_recv, w_send, x_recv, x_send, m_recv, m_send, t_recv, t_send,
-    d_recv, d_send, r_recv, r_send, rs_recv, rs_send,
+    f_recv, f_send, d_recv, d_send, r_recv, r_send, s1_recv, s1_send, s2_recv, s2_send_sem,
 ):
     dp = lax.axis_index("dp")
     e = lax.axis_index("expert")
     c = lax.rem(dp, 2)
     z = lax.rem(dp // 2, NZ)
     xl = dp // (2 * NZ)
-    oc = 1 - c
-    oxl = 1 - xl
+    xh, y = e // NY, lax.rem(e, NY)
+    x = xh * 2 + xl
+    oc, oxl = 1 - c, 1 - xl
 
     def dp_of(xl_, z_, c_):
         return (xl_ * NZ + z_) * 2 + c_
 
-    def dev(xl_, z_, c_, e_):
-        return {"dp": dp_of(xl_, z_, c_), "expert": e_}
-
-    sibling = dev(xl, z, oc, e)
-    ring = (dev(xl, mod(z + 1, NZ), c, e), dev(xl, mod(z - 1, NZ), c, e))
+    def dev(x_, y_, z_, c_):
+        return {"dp": dp_of(lax.rem(x_, 2), z_, c_), "expert": (x_ // 2) * NY + y_}
+
+    sibling = dev(x, y, z, oc)
+    ring = (dev(x, y, mod(z + 1, NZ), c), dev(x, y, mod(z - 1, NZ), c))
+    across = dev(xh * 2 + 1 - xl, y, z, c)
+    far_xpos = NX - 1 - x
+    far = dev(far_xpos, y, z, c)
     me16 = e * 2 + c
-    me32 = (xl * 2 + c) * NE + e
-
-    def peer16(m):
-        e_ = m // 2
-        xl_ = jnp.where(e_ // (NE // 2) == e // (NE // 2), xl, oxl)
-        return dev(xl_, z, lax.rem(m, 2), e_)
-
-    def peer32(m):
-        return dev(m // (2 * NE), z, lax.rem(m // NE, 2), lax.rem(m, NE))
+    me8 = y * 2 + c
+    near = [(1, 0), (3, 0), (2, 0), (1, 1), (3, 1), (2, 1), (0, 1)]
+
+    def near_at(dy, dc):
+        return lax.rem(y + dy, NY), (oc if dc else c)
 
     def remote(src, dst, send, recv, device):
         return pltpu.make_async_remote_copy(
@@ -79,14 +85,15 @@
         )
 
     barrier = pltpu.get_barrier_semaphore()
-    for d in range(2):
-        pl.semaphore_signal(barrier, inc=1, device_id=ring[d], device_id_type=MESH)
-
-    @pl.loop(1, GROUP)
-    def _(k):
-        pl.semaphore_signal(
-            barrier, inc=1, device_id=peer32(lax.rem(me32 + k, GROUP)), device_id_type=MESH
-        )
+    friends = list(ring)
+    for dx in range(1, NX):
+        friends.append(dev(lax.rem(x + dx, NX), y, z, c))
+    for dy, dc in near:
+        y_, c_ = near_at(dy, dc)
+        friends.append(dev(x, y_, z, c_))
+        friends.append(dev(far_xpos, y_, z, c_))
+    for friend in friends:
+        pl.semaphore_signal(barrier, inc=1, device_id=friend, device_id_type=MESH)
 
     def up_rows(dp_, count):
         return pl.ds(pl.multiple_of(dp_ * UPR, 16), count)
@@ -107,64 +114,57 @@
     for q in range(Q):
         gbuf[q, tok_rows(mine), :] = grad_ref[:, half_cols(c, q)]
 
-    ids = (emeta_ref[0:1, :], emeta_ref[1:2, :])
-    gates = (emeta_ref[2:3, :], emeta_ref[3:4, :])
     numbers = lax.broadcasted_iota(jnp.int32, (EXPERTS, TOK), 0).astype(F32)
     zeros = jnp.zeros((EXPERTS, TOK), F32)
-    hit0, hit1 = numbers == ids[0], numbers == ids[1]
-    hits = jnp.where(hit0 | hit1, 1.0, 0.0)
-    weight = jnp.where(hit0, gates[0], zeros) + jnp.where(hit1, gates[1], zeros)
     earlier = jnp.where(
         lax.broadcasted_iota(jnp.int32, (TOK, TOK), 0)
         < lax.broadcasted_iota(jnp.int32, (TOK, TOK), 1),
         1.0, 0.0,
     ).astype(BF16)
-    rank = jnp.dot(hits.astype(BF16), earlier, preferred_element_type=F32)
-    place = jnp.where(hits > 0.5, rank, -1.0)
     slots = lax.broadcasted_iota(jnp.int32, (CAP, TOK), 0).astype(F32)
-    for x in range(EXPERTS):
-        chosen = slots == place[x : x + 1, :]
-        pick[x * CAP : (x + 1) * CAP, :] = jnp.where(chosen, 1.0, 0.0).astype(BF16)
-        blend[x * CAP : (x + 1) * CAP, :] = jnp.where(chosen, weight[x : x + 1, :], 0.0)
-
-    own = me16 // 4
-
-    def dispatch(i):
-        first = lax.rem(own + i, 4) * 4
-        rows = pl.ds(pl.multiple_of(first * CAP, 128), 4 * CAP)
-        onehot = pick[rows, :]
+
+    def choose(meta, pick_ref, blend_ref):
+        hit0, hit1 = numbers == meta[0:1, :], numbers == meta[1:2, :]
+        hits = jnp.where(hit0 | hit1, 1.0, 0.0)
+        weight = jnp.where(hit0, meta[2:3, :], zeros) + jnp.where(hit1, meta[3:4, :], zeros)
+        rank = jnp.dot(hits.astype(BF16), earlier, preferred_element_type=F32)
+        place = jnp.where(hits > 0.5, rank, -1.0)
+        for n in range(EXPERTS):
+            chosen = slots == place[n : n + 1, :]
+            rows = slice(n * CAP, (n + 1) * CAP)
+            pick_ref[rows, :] = jnp.where(chosen, 1.0, 0.0).astype(BF16)
+            if blend_ref is not None:
+                blend_ref[rows, :] = jnp.where(chosen, weight[n : n + 1, :], 0.0)
+
+    def dispatch(group, array):
+        pick_ref = (pick, far_pick)[group]
+        src = ((input_ref, grad_ref), (far_x, far_g))[group][array]
+        out = (send_x, send_g)[array]
+        onehot = pick_ref[pl.ds(pl.multiple_of(xh * SET, SET), SET), :]
 
         @pl.loop(0, 5)
         def _(n):
             cols = pl.ds(pl.multiple_of(n * 512, 512), 512)
-            send_x[rows, cols] = jnp.dot(
-                onehot, input_ref[:, cols], preferred_element_type=F32
+            out[group * SET : (group + 1) * SET, cols] = jnp.dot(
+                onehot, src[:, cols], preferred_element_type=F32
             ).astype(BF16)
-            send_g[rows, cols] = jnp.dot(
-                onehot, grad_ref[:, cols], preferred_element_type=F32
-            ).astype(BF16)
-
-    def slot_rows(m):
-        return pl.ds(pl.multiple_of(m * CAP, CAP), CAP)
-
-    def dispatch_sends(i):
-        @pl.loop(0, 4)
-        def _(k):
-            m = lax.rem(own + i, 4) * 4 + lax.rem(me16 + k, 4)
-
-            @pl.when(m != me16)
-            def _():
-                remote(
-                    send_x.at[slot_rows(m)], got_x.at[slot_rows(me16)],
-                    d_send.at[0], d_recv.at[0], peer16(m),
-                ).start()
-                remote(
-                    send_g.at[slot_rows(m)], got_g.at[slot_rows(me16)],
-                    d_send.at[1], d_recv.at[1], peer16(m),
-                ).start()
-
-    dispatch(1)
-    pl.semaphore_wait(barrier, GROUP - 1 + 2)
+
+    def slot_rows(group, m):
+        return pl.ds(pl.multiple_of(group * SET + m * CAP, CAP), CAP)
+
+    def dispatch_sends(group, array):
+        out, got = ((send_x, got_x), (send_g, got_g))[array]
+        for dy, dc in near:
+            y_, c_ = near_at(dy, dc)
+            remote(
+                out.at[slot_rows(group, y_ * 2 + c_)], got.at[slot_rows(group, me8)],
+                d_send.at[group, array], d_recv.at[group, array], dev(x, y_, z, c_),
+            ).start()
+        got[slot_rows(group, me8), :] = out[slot_rows(group, me8), :]
+
+    choose(emeta_ref[...], pick, blend)
+    dispatch(0, 0)
+    pl.semaphore_wait(barrier, len(friends))
 
     pre = [
         remote(up_ref.at[oc], up_buf.at[up_rows(dp, UPR)], pre_send.at[0], pre_recv.at[0], sibling),
@@ -220,8 +220,6 @@
         send, recv = ring_sems(kind, d, s)
         remote(block, block, send, recv, ring[d]).wait_recv()
 
-    across = dev(oxl, z, c, e)
-
     def cross(d, zs):
         block = ring_block("weights", d, zs)
         remote(block, block, x_send.at[d], x_recv.at[d], across).start()
@@ -235,6 +233,10 @@
                 if kind == "weights":
                     cross(d, origin(d, s))
 
+    def far_copy(at):
+        src, dst = ((input_ref, far_x), (emeta_ref, far_meta), (grad_ref, far_g))[at]
+        return remote(src, dst, f_send.at[at], f_recv.at[at], far)
+
     remote(
         up_ref.at[c], up_buf.at[up_rows(dp, UPR)], w_send.at[0], w_recv.at[0, 0], ring[0]
     ).start()
@@ -243,10 +245,13 @@
     ).start()
     for copy in pre[:5]:
         copy.start()
+    for at in range(3):
+        far_copy(at).start()
     ring_send(0, 0, 0)
     ring_send(1, 0, 0)
-    dispatch_sends(1)
-    dispatch(2)
+    dispatch_sends(0, 0)
+    dispatch(0, 1)
+    dispatch_sends(0, 1)
     pre_wait(0)
     remote(
         arrivals[0], arrivals[0], w_send.at[0], w_recv.at[0, 0], ring[0]
@@ -263,17 +268,24 @@
     for q in range(2):
         pre_wait(3 + q)
         ring_send(q, 1, 0)
-    dispatch_sends(2)
     for copy in pre[5:]:
         copy.start()
-    for i in (3, 0):
-        dispatch(i)
-        dispatch_sends(i)
-    got_x[slot_rows(me16), :] = send_x[slot_rows(me16), :]
-    got_g[slot_rows(me16), :] = send_g[slot_rows(me16), :]
-
-    for s in range(1, NZ):
-        ring_step(("weights", 0, 1, "meta"), s)
+
+    first = ("weights", 0, 1, "meta")
+    ring_step(first, 1)
+    ring_step(first, 2)
+    far_copy(0).wait_recv()
+    far_copy(1).wait_recv()
+    choose(far_meta[...], far_pick, None)
+    dispatch(1, 0)
+    dispatch_sends(1, 0)
+    ring_step(first, 3)
+    ring_step(first, 4)
+    far_copy(2).wait_recv()
+    dispatch(1, 1)
+    dispatch_sends(1, 1)
+    for s in range(5, NZ):
+        ring_step(first, s)
     for q in range(2, Q):
         pre_wait(3 + q)
         for d in range(2):
@@ -282,10 +294,13 @@
     def all_bytes(ref, sem):
         pltpu.make_async_copy(ref, ref, sem).wait()
 
-    some = pl.ds(0, (EXPERTS - 1) * CAP)
-
-    def expert(i):
-        rows = pl.ds(i * 256, 256)
+    def others(group):
+        return pl.ds(group * SET, (PEERS - 1) * CAP)
+
+    def expert(group):
+        all_bytes(got_x.at[others(group)], d_recv.at[group, 0])
+        all_bytes(got_g.at[others(group)], d_recv.at[group, 1])
+        rows = pl.ds(group * SET, SET)
 
         @pl.loop(0, 2)
         def _(n):
@@ -300,16 +315,15 @@
             cols = pl.ds(pl.multiple_of(n * 256, 256), 256)
             ret_send[rows, cols] = nt_dot(slope_buf[...], up_buf[cols, :]).astype(BF16)
 
-        @pl.loop(0, 8)
-        def _(k):
-            m = i * 8 + lax.rem(me16 + k, 8)
-
-            @pl.when(m != me16)
-            def _():
-                remote(
-                    ret_send.at[slot_rows(m)], ret_got.at[slot_rows(me16)],
-                    r_send, r_recv, peer16(m),
-                ).start()
+        back_to = pl.ds(pl.multiple_of(me16 * CAP, CAP), CAP)
+        for dy, dc in near + ([(0, 0)] if group else []):
+            y_, c_ = near_at(dy, dc)
+            remote(
+                ret_send.at[slot_rows(group, y_ * 2 + c_)], ret_got.at[back_to],
+                r_send, r_recv, dev((x, far_xpos)[group], y_, z, c_),
+            ).start()
+        if group == 0:
+            ret_got[back_to, :] = ret_send[slot_rows(group, me8), :]
 
     targets = (lax.broadcasted_iota(jnp.int32, (TROWS, TOK), 0) + z * TROWS).astype(F32)
 
@@ -319,7 +333,10 @@
         one = jnp.where(targets == meta[1:2, :], meta[3:4, :], 0.0)
         sel[:, cols] = jnp.where(targets == meta[0:1, :], meta[2:3, :], one).astype(BF16)
 
-    def table_rows(m):
+    def x_rows(x_):
+        return pl.ds(pl.multiple_of(x_ * XROWS, XROWS), XROWS)
+
+    def m_rows(m):
         return pl.ds(pl.multiple_of(m * 32, 32), 32)
 
     def table_part(q):
@@ -330,22 +347,33 @@
                 sel[rows, :], gbuf[q], preferred_element_type=F32
             ).astype(BF16)
 
-        @pl.loop(1, GROUP)
-        def _(k):
-            m = lax.rem(me32 + k, GROUP)
+        for dx in (1, 3, 2):
+            x_ = lax.rem(x + dx, NX)
             remote(
-                dense.at[q, table_rows(m)], rs_got.at[q, (c * 2 + xl) * NE + e],
-                rs_send.at[q], rs_recv.at[q], peer32(m),
+                dense.at[q, x_rows(x_)], s1_got.at[q, dx - 1],
+                s1_send.at[q], s1_recv.at[q], dev(x_, y, z, c),
             ).start()
 
-        rs_got[q, (c * 2 + xl) * NE + e] = dense[q, table_rows(me32), :]
+    def table_mid(q):
+        all_bytes(s1_got.at[q], s1_recv.at[q])
+        total = dense[q, x_rows(x), :].astype(F32)
+        for k in range(NX - 1):
+            total += s1_got[q, k].astype(F32)
+        s2_send[q] = total.astype(BF16)
+        for dy, dc in near:
+            y_, c_ = near_at(dy, dc)
+            remote(
+                s2_send.at[q, m_rows(y_ * 2 + c_)], s2_got.at[q, c * NY + y],
+                s2_send_sem.at[q], s2_recv.at[q], dev(x, y_, z, c_),
+            ).start()
+        s2_got[q, c * NY + y] = s2_send[q, m_rows(me8), :]
 
     def table_sum(q):
-        all_bytes(rs_got.at[q, pl.ds(0, GROUP - 1)], rs_recv.at[q])
+        all_bytes(s2_got.at[q, pl.ds(0, PEERS - 1)], s2_recv.at[q])
         for order in range(2):
-            total = rs_got[q, order * 16].astype(F32)
-            for k in range(1, 16):
-                total += rs_got[q, order * 16 + k].astype(F32)
+            total = s2_got[q, order * NY].astype(F32)
+            for k in range(1, NY):
+                total += s2_got[q, order * NY + k].astype(F32)
             table_ref[order * 2 : order * 2 + 2, :, q * QW : (q + 1) * QW] = total.reshape(
                 2, 16, QW
             )
@@ -360,18 +388,17 @@
     ring_step(last, 3)
     all_bytes(up_buf.at[up_rows(dp_of(oxl, 0, 0), NZ * 2 * UPR)], x_recv.at[0])
     all_bytes(down_buf.at[down_rows(dp_of(oxl, 0, 0), NZ * 2 * DNR)], x_recv.at[1])
-    all_bytes(got_x.at[some], d_recv.at[0])
-    all_bytes(got_g.at[some], d_recv.at[1])
     expert(0)
     ring_step(last, 4)
     expert(1)
-    ret_got[slot_rows(me16), :] = ret_send[slot_rows(me16), :]
     for s in range(5, NZ):
         ring_step(last, s)
     for q in last:
         table_part(q)
-
-    all_bytes(ret_got.at[some], r_recv)
+    for q in range(Q):
+        table_mid(q)
+
+    all_bytes(ret_got.at[pl.ds(0, (EXPERTS - 1) * CAP)], r_recv)
     mix = blend[...].T.astype(BF16)
 
     @pl.loop(0, D // 256)
@@ -392,10 +419,14 @@
     all_bytes(mbuf.at[pl.ds(0, sends)], m_send)
     for q in range(Q):
         all_bytes(gbuf.at[q, pl.ds(0, sends * TOK)], t_send.at[q])
-        all_bytes(dense.at[q, pl.ds(0, (GROUP - 1) * 32)], rs_send.at[q])
-    all_bytes(send_x.at[some], d_send.at[0])
-    all_bytes(send_g.at[some], d_send.at[1])
-    all_bytes(ret_send.at[some], r_send)
+        all_bytes(s1_got.at[q], s1_send.at[q])
+        all_bytes(s2_got.at[q, pl.ds(0, PEERS - 1)], s2_send_sem.at[q])
+    for at in range(3):
+        far_copy(at).wait_send()
+    for group in range(2):
+        all_bytes(send_x.at[others(group)], d_send.at[group, 0])
+        all_bytes(send_g.at[others(group)], d_send.at[group, 1])
+    all_bytes(ret_send.at[pl.ds(0, (EXPERTS - 1) * CAP)], r_send)
 
 
 def per_device(
@@ -409,7 +440,9 @@
     core = memory_owner % 2
     zs = (memory_owner // 2) % NZ
     xs = memory_owner // (2 * NZ)
-    row = (((zs * XL + xs) * 2 + core) * NE + memory_slot // 16) * 32
+    to = memory_slot // 16
+    xs = (to // NY) * 2 + xs
+    row = (((zs * NX + xs) * NY + to % NY) * 2 + core) * 32
     row = row + head * 16 + memory_slot % 16
     rows_t = row.astype(F32).T.reshape(2, 2, TOK)
     gates_t = engram_gate.T.reshape(2, 2, TOK)
@@ -428,6 +461,10 @@
         scratch_shapes=[
             pltpu.VMEM((D, HID), BF16),
             pltpu.VMEM((HID, D), BF16),
+            pltpu.VMEM((TOK, D), BF16),
+            pltpu.VMEM((TOK, D), BF16),
+            pltpu.VMEM((8, TOK), F32),
+            pltpu.VMEM((EXPERTS * CAP, TOK), BF16),
             pltpu.VMEM((EXPERTS * CAP, TOK), BF16),
             pltpu.VMEM((EXPERTS * CAP, TOK), F32),
             pltpu.VMEM((EXPERTS * CAP, D), BF16),
@@ -441,7 +478,9 @@
             pltpu.VMEM((BLOCKS, 8, TOK), F32),
             pltpu.VMEM((TROWS, BLOCKS * TOK), BF16),
             pltpu.VMEM((Q, TROWS, QW), BF16),
-            pltpu.VMEM((Q, GROUP, 32, QW), BF16),
+            pltpu.VMEM((Q, NX - 1, XROWS, QW), BF16),
+            pltpu.VMEM((Q, XROWS, QW), BF16),
+            pltpu.VMEM((Q, PEERS, 32, QW), BF16),
             dma((3 + Q,)),
             dma((3 + Q,)),
             dma((2, NZ - 1)),
@@ -452,10 +491,14 @@
             dma(()),
             dma((2, Q, NZ - 1)),
             dma((Q,)),
-            dma((2,)),
-            dma((2,)),
+            dma((3,)),
+            dma((3,)),
+            dma((2, 2)),
+            dma((2, 2)),
             dma(()),
             dma(()),
+            dma((Q,)),
+            dma((Q,)),
             dma((Q,)),
             dma((Q,)),
         ],

time: 149 us -> 142 us (0.953)
  Pallas kernels: 143 us -> 135 us
    pallas_call x1, Pallas kernels: 143 us -> 135 us  [per_device(): pl.pallas_call(kernel, out_shape=(jax.ShapeDtypeStruct((TOK, D), BF16), j...]
where the time goes in v3:
time: 142 us; the launch traced here: 141 us
  Pallas kernels  135 us (95%)
  local copies, waits for them, and re-layouts  4.2 us (3%)
    pallas_call x1, Pallas kernels, per_device(): pl.pallas_call(kernel, out_shape=(jax.ShapeDtypeStruct((TOK, D), BF16), j...  135 us
    unnamed x14, local copies, waits for them, and re-layouts  4.12 us

profile of v3, /device:TPU:1, one launch (start us, length us, event | category | flops | bytes accessed | tf_op | source)
XLA Modules:
  0.0 141.5 jit_solution(16934542839102888125)
XLA Ops:
  0.6 0.0 copy-start.4
  0.7 0.0 copy-start.3
  0.7 0.1 pad.5.clone
  0.7 0.0 copy-start.2
  0.7 0.6 copy-done.4
  1.3 0.0 copy-done.3
  1.3 0.1 copy-done.2
  1.4 0.1 fusion.12
  1.5 0.0 copy-start.5
  1.5 0.7 copy-done.5
  2.2 0.0 copy-start.1
  2.2 0.7 maximum_maximum_fusion.1.emeta_ref
  2.8 0.0 copy-done.1
  2.9 0.7 maximum_maximum_fusion.mmeta_ref
  3.5 135.2 %shard_map.104 = (bf16[128,2560]{1,0:T(8,128)(2,1)}, f32[4,16,1280]{2,1,0:T(8,128)}) custom-call(bf16[128,2560]{1,0:T(8,128)(2,1)} %grad_ref.1, bf16[128,2560]{1,0:T(8,128)(2,1)} %input_ref.1, bf16[2,80,512]{2,1,0:T(8,128)(2,1)} %up_ref.1, bf16[2,16,2560]{2,1,0:T(8,128)(2,1)} %down_ref.1, f32[8,128]{1,0:T(8,128)} %maximum_maximum_fusion.1.emeta_ref, ...), custom_call_target="tpu_custom_call" | custom-call | flops 10000000000 | bytes 4000000 | tf_op jit(solution)/shard_map/pallas_call | solution.py:453
  138.7 0.0 copy-start
  138.7 2.0 %copy.13 = bf16[128,2560]{1,0:T(8,128)(2,1)} copy(bf16[128,2560]{1,0:T(8,128)(2,1)} %get-tuple-element.4) | data formatting | bytes 1310720
  140.7 0.0 copy-done
  140.7 0.7 copy.14
  (3 shorter events, 0.0 us)
Async XLA Ops:
  0.6 0.7 copy-start.4
  0.7 0.7 copy-start.3
  0.7 0.7 copy-start.2
  1.5 0.7 copy-start.5
  2.2 0.7 copy-start.1
  138.7 2.0 %copy-start = (f32[4,16,1280]{2,1,0:T(8,128)S(1)}, f32[4,16,1280]{2,1,0:T(8,128)}, u32[]{:S(2)}) copy-start(f32[4,16,1280]{2,1,0:T(8,128)} %get-tuple-element.5) | copy-start | bytes 983044

commit v4 on v3

--- a/solution.py
+++ b/solution.py
@@ -13,6 +13,7 @@
 NZ = 8
 XL = 2
 CORES = 2
+FAR_Z = NZ // 2
 XH = 2
 NY = 4
 NE = XH * NY
@@ -43,13 +44,13 @@
 
 
 def kernel(
-    grad_ref, input_ref, up_ref, down_ref, emeta_ref, mmeta_ref,
+    grad_ref, input_ref, up_ref, down_ref, meta_ref,
     gi_ref, table_ref,
-    up_buf, down_buf, far_x, far_g, far_meta, pick, far_pick, blend,
-    send_x, send_g, got_x, got_g, slope_buf, ret_send, ret_got,
+    up_buf, down_buf, far_x, far_g, far_meta, pick, far_pick, blend, far_blend,
+    send_x, send_g, got_x, got_g, slope_buf, ret_send, ret_got, far_out, far_back,
     gbuf, mbuf, sel, dense, s1_got, s2_send, s2_got,
-    pre_recv, pre_send, w_recv, w_send, x_recv, x_send, m_recv, m_send, t_recv, t_send,
-    f_recv, f_send, d_recv, d_send, r_recv, r_send, s1_recv, s1_send, s2_recv, s2_send_sem,
+    pre_recv, pre_send, w_recv, w_send, x_recv, x2_recv, x_send, e_recv, e_send, m_recv, m_send, t_recv, t_send,
+    f_recv, f_send, d_recv, d_send, r_recv, r_send, b_recv, b_send, s1_recv, s1_send, s2_recv, s2_send_sem,
 ):
     dp = lax.axis_index("dp")
     e = lax.axis_index("expert")
@@ -69,9 +70,7 @@
     sibling = dev(x, y, z, oc)
     ring = (dev(x, y, mod(z + 1, NZ), c), dev(x, y, mod(z - 1, NZ), c))
     across = dev(xh * 2 + 1 - xl, y, z, c)
-    far_xpos = NX - 1 - x
-    far = dev(far_xpos, y, z, c)
-    me16 = e * 2 + c
+    far = dev(NX - 1 - x, y, z, c)
     me8 = y * 2 + c
     near = [(1, 0), (3, 0), (2, 0), (1, 1), (3, 1), (2, 1), (0, 1)]
 
@@ -91,7 +90,6 @@
     for dy, dc in near:
         y_, c_ = near_at(dy, dc)
         friends.append(dev(x, y_, z, c_))
-        friends.append(dev(far_xpos, y_, z, c_))
     for friend in friends:
         pl.semaphore_signal(barrier, inc=1, device_id=friend, device_id_type=MESH)
 
@@ -110,7 +108,7 @@
     up_buf[up_rows(dp, UPR), :] = up_ref[c]
     down_buf[down_rows(dp, DNR), :] = down_ref[c]
     mine, theirs = z * 2 + c, z * 2 + oc
-    mbuf[mine] = mmeta_ref[c]
+    mbuf[mine] = meta_ref[c]
     for q in range(Q):
         gbuf[q, tok_rows(mine), :] = grad_ref[:, half_cols(c, q)]
 
@@ -133,8 +131,7 @@
             chosen = slots == place[n : n + 1, :]
             rows = slice(n * CAP, (n + 1) * CAP)
             pick_ref[rows, :] = jnp.where(chosen, 1.0, 0.0).astype(BF16)
-            if blend_ref is not None:
-                blend_ref[rows, :] = jnp.where(chosen, weight[n : n + 1, :], 0.0)
+            blend_ref[rows, :] = jnp.where(chosen, weight[n : n + 1, :], 0.0)
 
     def dispatch(group, array):
         pick_ref = (pick, far_pick)[group]
@@ -162,7 +159,7 @@
             ).start()
         got[slot_rows(group, me8), :] = out[slot_rows(group, me8), :]
 
-    choose(emeta_ref[...], pick, blend)
+    choose(meta_ref[2], pick, blend)
     dispatch(0, 0)
     pl.semaphore_wait(barrier, len(friends))
 
@@ -172,7 +169,7 @@
             down_ref.at[oc], down_buf.at[down_rows(dp, DNR)],
             pre_send.at[1], pre_recv.at[1], sibling,
         ),
-        remote(mmeta_ref.at[oc], mbuf.at[mine], pre_send.at[2], pre_recv.at[2], sibling),
+        remote(meta_ref.at[oc], mbuf.at[mine], pre_send.at[2], pre_recv.at[2], sibling),
     ]
     for q in range(Q):
         pre.append(remote(
@@ -193,103 +190,97 @@
     def origin(d, s):
         return mod(z - s, NZ) if d == 0 else mod(z + s, NZ)
 
-    def ring_block(kind, d, zs):
+    def weight_rows(at, xl_, zs):
+        dp_ = dp_of(xl_, zs, 0)
+        if at == 0:
+            return up_buf.at[up_rows(dp_, 2 * UPR)]
+        return down_buf.at[down_rows(dp_, 2 * DNR)]
+
+    def ring_parts(kind, d, s, half):
+        zs = origin(d, s)
         if kind == "weights":
-            if d == 0:
-                return up_buf.at[up_rows(dp_of(xl, zs, 0), 2 * UPR)]
-            return down_buf.at[down_rows(dp_of(xl, zs, 0), 2 * DNR)]
-        block = zs * 2 + (c, oc)[d]
+            return [
+                (weight_rows(at, xl, zs), w_send.at[at], w_recv.at[d, at])
+                for at in ((d,) if half else (0, 1))
+            ]
+        block, count = (zs * 2 + d, 1) if half else (zs * 2, 2)
         if kind == "meta":
-            return mbuf.at[block]
-        return gbuf.at[kind, tok_rows(block)]
-
-    def ring_sems(kind, d, s):
-        if kind == "weights":
-            return w_send.at[d], w_recv.at[d, s]
-        if kind == "meta":
-            return m_send, m_recv.at[d, s]
-        return t_send.at[kind], t_recv.at[d, kind, s]
+            return [(mbuf.at[pl.ds(block, count)], m_send, m_recv.at[d])]
+        rows = pl.ds(pl.multiple_of(block * TOK, TOK), count * TOK)
+        return [(gbuf.at[kind, rows], t_send.at[kind], t_recv.at[d, kind])]
 
     def ring_send(kind, d, s):
-        block = ring_block(kind, d, origin(d, s))
-        send, recv = ring_sems(kind, d, s)
-        remote(block, block, send, recv, ring[d]).start()
-
-    def ring_wait(kind, d, s):
-        block = ring_block(kind, d, origin(d, s + 1))
-        send, recv = ring_sems(kind, d, s)
-        remote(block, block, send, recv, ring[d]).wait_recv()
-
-    def cross(d, zs):
-        block = ring_block("weights", d, zs)
-        remote(block, block, x_send.at[d], x_recv.at[d], across).start()
-
-    def ring_step(kinds, s):
-        for kind in kinds:
-            for d in range(2):
-                ring_wait(kind, d, s - 1)
-                if s < NZ - 1:
-                    ring_send(kind, d, s)
-                if kind == "weights":
-                    cross(d, origin(d, s))
+        for block, send, recv in ring_parts(kind, d, s, s == FAR_Z - 1):
+            remote(block, block, send, recv.at[s], ring[d]).start()
+
+    def cross(block, at, recv):
+        remote(block, block, x_send.at[at], recv, across).start()
+
+    def ring_step(kind, s):
+        for d in range(2):
+            for block, send, recv in ring_parts(kind, d, s, s == FAR_Z):
+                remote(block, block, send, recv.at[s - 1], ring[d]).wait_recv()
+            if s < FAR_Z:
+                ring_send(kind, d, s)
+            if kind == "weights" and s != FAR_Z - 1:
+                for at in (d,) if s == FAR_Z else (0, 1):
+                    recv = x2_recv.at[at, d] if s == FAR_Z - 2 else x_recv.at[at]
+                    cross(weight_rows(at, xl, origin(d, s)), at, recv)
+
+    def wide_copy(d, at, s):
+        block = weight_rows(at, oxl, origin(d, s))
+        return remote(block, block, e_send.at[d, at], e_recv.at[d, at], ring[d])
+
+    def wide_send(d):
+        for at in range(2):
+            block = weight_rows(at, oxl, origin(d, FAR_Z - 2))
+            remote(block, block, x_send.at[at], x2_recv.at[at, d], across).wait_recv()
+            wide_copy(d, at, FAR_Z - 2).start()
+
+    def piece(q):
+        pre_wait(3 + q)
+        for d in range(2):
+            ring_send(q, d, 0)
+
+    def steps(*pairs):
+        for kind, at in pairs:
+            ring_step(kind, at)
 
     def far_copy(at):
-        src, dst = ((input_ref, far_x), (emeta_ref, far_meta), (grad_ref, far_g))[at]
+        src, dst = ((input_ref, far_x), (meta_ref.at[2], far_meta), (grad_ref, far_g))[at]
         return remote(src, dst, f_send.at[at], f_recv.at[at], far)
 
-    remote(
-        up_ref.at[c], up_buf.at[up_rows(dp, UPR)], w_send.at[0], w_recv.at[0, 0], ring[0]
-    ).start()
-    remote(
-        down_ref.at[c], down_buf.at[down_rows(dp, DNR)], w_send.at[1], w_recv.at[1, 0], ring[1]
-    ).start()
-    for copy in pre[:5]:
+    def set_out(at, block):
+        for d in range(2):
+            remote(block, block, w_send.at[at], w_recv.at[d, at, 0], ring[d]).start()
+        cross(block, at, x_recv.at[at])
+
+    for copy in pre[:3]:
         copy.start()
+    set_out(0, up_buf.at[up_rows(dp, UPR)])
+    set_out(1, down_buf.at[down_rows(dp, DNR)])
     for at in range(3):
         far_copy(at).start()
-    ring_send(0, 0, 0)
-    ring_send(1, 0, 0)
+    pre_wait(0)
+    set_out(0, arrivals[0])
+    pre_wait(1)
+    set_out(1, arrivals[1])
     dispatch_sends(0, 0)
-    dispatch(0, 1)
-    dispatch_sends(0, 1)
-    pre_wait(0)
-    remote(
-        arrivals[0], arrivals[0], w_send.at[0], w_recv.at[0, 0], ring[0]
-    ).start()
-    cross(0, z)
-    pre_wait(1)
-    remote(
-        arrivals[1], arrivals[1], w_send.at[1], w_recv.at[1, 0], ring[1]
-    ).start()
-    cross(1, z)
     pre_wait(2)
     for d in range(2):
         ring_send("meta", d, 0)
-    for q in range(2):
-        pre_wait(3 + q)
-        ring_send(q, 1, 0)
-    for copy in pre[5:]:
+    dispatch(0, 1)
+    dispatch_sends(0, 1)
+    for copy in pre[3:]:
         copy.start()
 
-    first = ("weights", 0, 1, "meta")
-    ring_step(first, 1)
-    ring_step(first, 2)
-    far_copy(0).wait_recv()
-    far_copy(1).wait_recv()
-    choose(far_meta[...], far_pick, None)
-    dispatch(1, 0)
-    dispatch_sends(1, 0)
-    ring_step(first, 3)
-    ring_step(first, 4)
-    far_copy(2).wait_recv()
-    dispatch(1, 1)
-    dispatch_sends(1, 1)
-    for s in range(5, NZ):
-        ring_step(first, s)
-    for q in range(2, Q):
-        pre_wait(3 + q)
-        for d in range(2):
-            ring_send(q, d, 0)
+    targets = (lax.broadcasted_iota(jnp.int32, (TROWS, TOK), 0) + z * TROWS).astype(F32)
+
+    def select(block):
+        cols = pl.ds(pl.multiple_of(block * TOK, TOK), TOK)
+        meta = mbuf[block]
+        one = jnp.where(targets == meta[1:2, :], meta[3:4, :], 0.0)
+        sel[:, cols] = jnp.where(targets == meta[0:1, :], meta[2:3, :], one).astype(BF16)
 
     def all_bytes(ref, sem):
         pltpu.make_async_copy(ref, ref, sem).wait()
@@ -297,7 +288,7 @@
     def others(group):
         return pl.ds(group * SET, (PEERS - 1) * CAP)
 
-    def expert(group):
+    def expert_in(group):
         all_bytes(got_x.at[others(group)], d_recv.at[group, 0])
         all_bytes(got_g.at[others(group)], d_recv.at[group, 1])
         rows = pl.ds(group * SET, SET)
@@ -310,28 +301,49 @@
             sig = 1.0 / (1.0 + jnp.exp(-before))
             slope_buf[:, cols] = (back * sig * (1.0 + before * (1.0 - sig))).astype(BF16)
 
-        @pl.loop(0, D // 256)
+    def expert_out(group, part):
+        rows = pl.ds(group * SET, SET)
+
+        @pl.loop(part * 5, part * 5 + 5)
         def _(n):
             cols = pl.ds(pl.multiple_of(n * 256, 256), 256)
             ret_send[rows, cols] = nt_dot(slope_buf[...], up_buf[cols, :]).astype(BF16)
 
-        back_to = pl.ds(pl.multiple_of(me16 * CAP, CAP), CAP)
-        for dy, dc in near + ([(0, 0)] if group else []):
+        cols = slice(part * HALF, (part + 1) * HALF)
+        for dy, dc in near:
             y_, c_ = near_at(dy, dc)
             remote(
-                ret_send.at[slot_rows(group, y_ * 2 + c_)], ret_got.at[back_to],
-                r_send, r_recv, dev((x, far_xpos)[group], y_, z, c_),
+                ret_send.at[slot_rows(group, y_ * 2 + c_), cols],
+                ret_got.at[slot_rows(group, me8), cols],
+                r_send.at[group, part], r_recv.at[group, part], dev(x, y_, z, c_),
             ).start()
-        if group == 0:
-            ret_got[back_to, :] = ret_send[slot_rows(group, me8), :]
-
-    targets = (lax.broadcasted_iota(jnp.int32, (TROWS, TOK), 0) + z * TROWS).astype(F32)
-
-    def select(block):
-        cols = pl.ds(pl.multiple_of(block * TOK, TOK), TOK)
-        meta = mbuf[block]
-        one = jnp.where(targets == meta[1:2, :], meta[3:4, :], 0.0)
-        sel[:, cols] = jnp.where(targets == meta[0:1, :], meta[2:3, :], one).astype(BF16)
+        ret_got[slot_rows(group, me8), cols] = ret_send[slot_rows(group, me8), cols]
+
+    def returned(group, part):
+        cols = pl.ds(part * HALF, HALF)
+        all_bytes(ret_got.at[others(group), cols], r_recv.at[group, part])
+
+    def mix_of(blend_ref):
+        return blend_ref[pl.ds(pl.multiple_of(xh * SET, SET), SET), :].T.astype(BF16)
+
+    def back_copy(part):
+        cols = pl.ds(part * HALF, HALF)
+        return remote(
+            far_out.at[:, cols], far_back.at[:, cols], b_send.at[part], b_recv.at[part], far
+        )
+
+    def far_combine(part):
+        returned(1, part)
+        mix = mix_of(far_blend)
+
+        @pl.loop(part * 5, part * 5 + 5)
+        def _(n):
+            cols = pl.ds(pl.multiple_of(n * 256, 256), 256)
+            far_out[:, cols] = jnp.dot(
+                mix, ret_got[SET : 2 * SET, cols], preferred_element_type=F32
+            ).astype(BF16)
+
+        back_copy(part).start()
 
     def x_rows(x_):
         return pl.ds(pl.multiple_of(x_ * XROWS, XROWS), XROWS)
@@ -378,44 +390,92 @@
                 2, 16, QW
             )
 
-    last = tuple(range(2, Q))
-    pl.loop(0, BLOCKS // 2)(select)
-    ring_step(last, 1)
-    pl.loop(BLOCKS // 2, BLOCKS)(select)
-    ring_step(last, 2)
-    table_part(0)
-    table_part(1)
-    ring_step(last, 3)
-    all_bytes(up_buf.at[up_rows(dp_of(oxl, 0, 0), NZ * 2 * UPR)], x_recv.at[0])
-    all_bytes(down_buf.at[down_rows(dp_of(oxl, 0, 0), NZ * 2 * DNR)], x_recv.at[1])
-    expert(0)
-    ring_step(last, 4)
-    expert(1)
-    for s in range(5, NZ):
-        ring_step(last, s)
-    for q in last:
+    def sources(s):
+        for d in range(2):
+            for core in range(2) if s < FAR_Z else (d,):
+                select(origin(d, s) * 2 + core)
+
+    steps(("weights", 1), ("meta", 1))
+    select(mine)
+    select(theirs)
+    sources(1)
+    steps(("weights", 2), ("meta", 2))
+    far_copy(0).wait_recv()
+    far_copy(1).wait_recv()
+    choose(far_meta[...], far_pick, far_blend)
+    dispatch(1, 0)
+    dispatch_sends(1, 0)
+    steps(("weights", 3), ("meta", 3))
+    for q in range(3):
+        piece(q)
+    sources(2)
+    far_copy(2).wait_recv()
+    dispatch(1, 1)
+    dispatch_sends(1, 1)
+    steps(("weights", 4), ("meta", 4))
+    wide_send(0)
+    wide_send(1)
+    steps((0, 1), (1, 1), (2, 1))
+    sources(3)
+    sources(4)
+    all_bytes(up_buf.at[pl.ds(0, 4 * 2 * UPR)], x_recv.at[0])
+    all_bytes(down_buf.at[pl.ds(0, 4 * 2 * DNR)], x_recv.at[1])
+    for d in range(2):
+        for at in range(2):
+            wide_copy(d, at, FAR_Z - 1).wait_recv()
+    expert_in(0)
+    steps((0, 2), (1, 2), (2, 2))
+    expert_out(0, 0)
+    expert_out(0, 1)
+    steps((0, 3), (1, 3), (2, 3))
+    piece(3)
+    piece(4)
+    expert_in(1)
+    expert_out(1, 0)
+    expert_out(1, 1)
+    for q in range(3):
+        ring_step(q, 4)
         table_part(q)
-    for q in range(Q):
-        table_mid(q)
-
-    all_bytes(ret_got.at[pl.ds(0, (EXPERTS - 1) * CAP)], r_recv)
-    mix = blend[...].T.astype(BF16)
-
-    @pl.loop(0, D // 256)
-    def _(n):
-        cols = pl.ds(pl.multiple_of(n * 256, 256), 256)
-        gi_ref[:, cols] = jnp.dot(mix, ret_got[:, cols], preferred_element_type=F32).astype(BF16)
-
-    for q in range(Q):
+    steps((3, 1), (4, 1))
+    far_combine(0)
+    steps((3, 2), (4, 2))
+    table_mid(0)
+    far_combine(1)
+    steps((3, 3), (4, 3))
+    table_mid(1)
+    table_mid(2)
+    for q in (3, 4):
+        ring_step(q, 4)
+        table_part(q)
+
+    mix = mix_of(blend)
+    for part in range(2):
+        returned(0, part)
+        back_copy(part).wait_recv()
+
+        @pl.loop(part * 5, part * 5 + 5)
+        def _(n):
+            cols = pl.ds(pl.multiple_of(n * 256, 256), 256)
+            total = jnp.dot(mix, ret_got[0:SET, cols], preferred_element_type=F32)
+            gi_ref[:, cols] = (total + far_back[:, cols].astype(F32)).astype(BF16)
+
+    for q in range(3):
         table_sum(q)
+    table_mid(3)
+    table_mid(4)
+    table_sum(3)
+    table_sum(4)
 
     for copy in pre:
         copy.wait_send()
     sends = 2 * (NZ - 1)
     all_bytes(up_buf.at[pl.ds(0, (NZ - 1) * 2 * UPR)], w_send.at[0])
     all_bytes(down_buf.at[pl.ds(0, (NZ - 1) * 2 * DNR)], w_send.at[1])
-    all_bytes(up_buf.at[pl.ds(0, NZ * 2 * UPR)], x_send.at[0])
-    all_bytes(down_buf.at[pl.ds(0, NZ * 2 * DNR)], x_send.at[1])
+    all_bytes(up_buf.at[pl.ds(0, 6 * 2 * UPR)], x_send.at[0])
+    all_bytes(down_buf.at[pl.ds(0, 6 * 2 * DNR)], x_send.at[1])
+    for d in range(2):
+        for at in range(2):
+            wide_copy(d, at, FAR_Z - 2).wait_send()
     all_bytes(mbuf.at[pl.ds(0, sends)], m_send)
     for q in range(Q):
         all_bytes(gbuf.at[q, pl.ds(0, sends * TOK)], t_send.at[q])
@@ -426,16 +486,16 @@
     for group in range(2):
         all_bytes(send_x.at[others(group)], d_send.at[group, 0])
         all_bytes(send_g.at[others(group)], d_send.at[group, 1])
-    all_bytes(ret_send.at[pl.ds(0, (EXPERTS - 1) * CAP)], r_send)
+        for part in range(2):
+            all_bytes(ret_send.at[others(group), pl.ds(part * HALF, HALF)], r_send.at[group, part])
+    for part in range(2):
+        back_copy(part).wait_send()
 
 
 def per_device(
     grad_out, saved_input, expert_ids, gate_weights, up_weight, down_weight,
     engram_gate, memory_owner, memory_slot,
 ):
-    emeta = jnp.concatenate(
-        [expert_ids.astype(F32).T, gate_weights.T, jnp.zeros((4, TOK), F32)], axis=0
-    )
     head = jnp.arange(4, dtype=jnp.int32)[None, :] % 2
     core = memory_owner % 2
     zs = (memory_owner // 2) % NZ
@@ -444,9 +504,16 @@
     xs = (to // NY) * 2 + xs
     row = (((zs * NX + xs) * NY + to % NY) * 2 + core) * 32
     row = row + head * 16 + memory_slot % 16
-    rows_t = row.astype(F32).T.reshape(2, 2, TOK)
-    gates_t = engram_gate.T.reshape(2, 2, TOK)
-    mmeta = jnp.concatenate([rows_t, gates_t, jnp.zeros((2, 4, TOK), F32)], axis=1)
+    rows = jnp.concatenate([row, expert_ids], axis=1).astype(F32)
+    gates = jnp.concatenate([engram_gate, gate_weights], axis=1)
+    meta = jnp.concatenate(
+        [
+            rows.T.reshape(3, 2, TOK),
+            gates.T.reshape(3, 2, TOK),
+            jnp.zeros((3, 4, TOK), F32),
+        ],
+        axis=1,
+    )
 
     vmem = pl.BlockSpec(memory_space=pltpu.VMEM)
     dma = pltpu.SemaphoreType.DMA
@@ -456,7 +523,7 @@
             jax.ShapeDtypeStruct((TOK, D), BF16),
             jax.ShapeDtypeStruct((4, 16, HALF), F32),
         ),
-        in_specs=[vmem] * 6,
+        in_specs=[vmem] * 5,
         out_specs=(vmem, vmem),
         scratch_shapes=[
             pltpu.VMEM((D, HID), BF16),
@@ -467,6 +534,7 @@
             pltpu.VMEM((EXPERTS * CAP, TOK), BF16),
             pltpu.VMEM((EXPERTS * CAP, TOK), BF16),
             pltpu.VMEM((EXPERTS * CAP, TOK), F32),
+            pltpu.VMEM((EXPERTS * CAP, TOK), F32),
             pltpu.VMEM((EXPERTS * CAP, D), BF16),
             pltpu.VMEM((EXPERTS * CAP, D), BF16),
             pltpu.VMEM((EXPERTS * CAP, D), BF16),
@@ -474,6 +542,8 @@
             pltpu.VMEM((256, HID), BF16),
             pltpu.VMEM((EXPERTS * CAP, D), BF16),
             pltpu.VMEM((EXPERTS * CAP, D), BF16),
+            pltpu.VMEM((TOK, D), BF16),
+            pltpu.VMEM((TOK, D), BF16),
             pltpu.VMEM((Q, BLOCKS * TOK, QW), BF16),
             pltpu.VMEM((BLOCKS, 8, TOK), F32),
             pltpu.VMEM((TROWS, BLOCKS * TOK), BF16),
@@ -483,20 +553,25 @@
             pltpu.VMEM((Q, PEERS, 32, QW), BF16),
             dma((3 + Q,)),
             dma((3 + Q,)),
-            dma((2, NZ - 1)),
+            dma((2, 2, FAR_Z)),
             dma((2,)),
             dma((2,)),
+            dma((2, 2)),
             dma((2,)),
-            dma((2, NZ - 1)),
+            dma((2, 2)),
+            dma((2, 2)),
+            dma((2, FAR_Z)),
             dma(()),
-            dma((2, Q, NZ - 1)),
+            dma((2, Q, FAR_Z)),
             dma((Q,)),
             dma((3,)),
             dma((3,)),
             dma((2, 2)),
             dma((2, 2)),
-            dma(()),
-            dma(()),
+            dma((2, 2)),
+            dma((2, 2)),
+            dma((2,)),
+            dma((2,)),
             dma((Q,)),
             dma((Q,)),
             dma((Q,)),
@@ -508,7 +583,7 @@
         cost_estimate=pl.CostEstimate(
             flops=10_000_000_000, bytes_accessed=4_000_000, transcendentals=262_144
         ),
-    )(grad_out, saved_input, up_weight, down_weight, emeta, mmeta)
+    )(grad_out, saved_input, up_weight, down_weight, meta)
 
 
 def solution(mesh):

time: 142 us -> 134 us (0.944)
  Pallas kernels: 135 us -> 127 us
    pallas_call x1, Pallas kernels: 135 us -> 127 us  [per_device(): pl.pallas_call(kernel, out_shape=(jax.ShapeDtypeStruct((TOK, D), BF16), j...]
where the time goes in v4:
time: 134 us
  Pallas kernels  127 us (95%)
  local copies, waits for them, and re-layouts  4.72 us (4%)
    pallas_call x1, Pallas kernels, per_device(): pl.pallas_call(kernel, out_shape=(jax.ShapeDtypeStruct((TOK, D), BF16), j...  127 us
    unnamed x14, local copies, waits for them, and re-layouts  4.62 us

profile of v4, /device:TPU:1, one launch (start us, length us, event | category | flops | bytes accessed | tf_op | source)
XLA Modules:
  0.0 133.6 jit_solution(2677570174548445020)
XLA Ops:
  0.6 0.0 copy-start.3
  0.6 0.0 copy-start.2
  0.7 0.1 pad.2.clone
  0.7 0.6 copy-done.3
  1.3 0.0 copy-done.2
  1.3 0.0 copy-start.4
  1.3 0.1 fusion.12
  1.4 0.6 copy-done.4
  2.0 0.0 copy-start.1
  2.0 0.0 copy-start.5
  2.1 0.7 copy-done.1
  2.7 0.0 copy-done.5
  2.7 0.7 maximum_maximum_fusion.meta_ref
  3.4 127.4 %shard_map.104 = (bf16[128,2560]{1,0:T(8,128)(2,1)}, f32[4,16,1280]{2,1,0:T(8,128)}) custom-call(bf16[128,2560]{1,0:T(8,128)(2,1)} %grad_ref.1, bf16[128,2560]{1,0:T(8,128)(2,1)} %input_ref.1, bf16[2,80,512]{2,1,0:T(8,128)(2,1)} %up_ref.1, bf16[2,16,2560]{2,1,0:T(8,128)(2,1)} %down_ref.1, f32[3,8,128]{2,1,0:T(8,128)} %maximum_maximum_fusion.meta_ref), custom_call_target="tpu_custom_call" | custom-call | flops 10000000000 | bytes 4000000 | tf_op jit(solution)/shard_map/pallas_call | solution.py:520
  130.8 0.0 copy-start
  130.8 2.0 %copy.13 = bf16[128,2560]{1,0:T(8,128)(2,1)} copy(bf16[128,2560]{1,0:T(8,128)(2,1)} %get-tuple-element.4) | data formatting | bytes 1310720
  132.8 0.0 copy-done
  132.8 0.7 copy.14
  (6 shorter events, 0.0 us)
Async XLA Ops:
  0.6 0.7 copy-start.3
  0.6 0.7 copy-start.2
  1.3 0.7 copy-start.4
  2.0 0.7 copy-start.1
  2.0 0.7 copy-start.5
  130.8 2.0 %copy-start = (f32[4,16,1280]{2,1,0:T(8,128)S(1)}, f32[4,16,1280]{2,1,0:T(8,128)}, u32[]{:S(2)}) copy-start(f32[4,16,1280]{2,1,0:T(8,128)} %get-tuple-element.5) | copy-start | bytes 983044

commit v5 on v4

--- a/solution.py
+++ b/solution.py
@@ -255,23 +255,21 @@
             remote(block, block, w_send.at[at], w_recv.at[d, at, 0], ring[d]).start()
         cross(block, at, x_recv.at[at])
 
-    for copy in pre[:3]:
+    for copy in pre[:4]:
         copy.start()
+    for at in range(3):
+        far_copy(at).start()
     set_out(0, up_buf.at[up_rows(dp, UPR)])
     set_out(1, down_buf.at[down_rows(dp, DNR)])
-    for at in range(3):
-        far_copy(at).start()
+    dispatch_sends(0, 0)
     pre_wait(0)
     set_out(0, arrivals[0])
     pre_wait(1)
     set_out(1, arrivals[1])
-    dispatch_sends(0, 0)
     pre_wait(2)
     for d in range(2):
         ring_send("meta", d, 0)
-    dispatch(0, 1)
-    dispatch_sends(0, 1)
-    for copy in pre[3:]:
+    for copy in pre[4:]:
         copy.start()
 
     targets = (lax.broadcasted_iota(jnp.int32, (TROWS, TOK), 0) + z * TROWS).astype(F32)
@@ -299,7 +297,7 @@
             before = jnp.dot(got_x[rows, :], up_buf[:, cols], preferred_element_type=F32)
             back = nt_dot(got_g[rows, :], down_buf[cols, :])
             sig = 1.0 / (1.0 + jnp.exp(-before))
-            slope_buf[:, cols] = (back * sig * (1.0 + before * (1.0 - sig))).astype(BF16)
+            slope_buf[group, :, cols] = (back * sig * (1.0 + before * (1.0 - sig))).astype(BF16)
 
     def expert_out(group, part):
         rows = pl.ds(group * SET, SET)
@@ -307,8 +305,9 @@
         @pl.loop(part * 5, part * 5 + 5)
         def _(n):
             cols = pl.ds(pl.multiple_of(n * 256, 256), 256)
-            ret_send[rows, cols] = nt_dot(slope_buf[...], up_buf[cols, :]).astype(BF16)
-
+            ret_send[rows, cols] = nt_dot(slope_buf[group], up_buf[cols, :]).astype(BF16)
+
+    def expert_send(group, part):
         cols = slice(part * HALF, (part + 1) * HALF)
         for dy, dc in near:
             y_, c_ = near_at(dy, dc)
@@ -395,61 +394,35 @@
             for core in range(2) if s < FAR_Z else (d,):
                 select(origin(d, s) * 2 + core)
 
-    steps(("weights", 1), ("meta", 1))
-    select(mine)
-    select(theirs)
-    sources(1)
-    steps(("weights", 2), ("meta", 2))
-    far_copy(0).wait_recv()
-    far_copy(1).wait_recv()
-    choose(far_meta[...], far_pick, far_blend)
-    dispatch(1, 0)
-    dispatch_sends(1, 0)
-    steps(("weights", 3), ("meta", 3))
-    for q in range(3):
-        piece(q)
-    sources(2)
-    far_copy(2).wait_recv()
-    dispatch(1, 1)
-    dispatch_sends(1, 1)
-    steps(("weights", 4), ("meta", 4))
-    wide_send(0)
-    wide_send(1)
-    steps((0, 1), (1, 1), (2, 1))
-    sources(3)
-    sources(4)
-    all_bytes(up_buf.at[pl.ds(0, 4 * 2 * UPR)], x_recv.at[0])
-    all_bytes(down_buf.at[pl.ds(0, 4 * 2 * DNR)], x_recv.at[1])
-    for d in range(2):
-        for at in range(2):
-            wide_copy(d, at, FAR_Z - 1).wait_recv()
-    expert_in(0)
-    steps((0, 2), (1, 2), (2, 2))
-    expert_out(0, 0)
-    expert_out(0, 1)
-    steps((0, 3), (1, 3), (2, 3))
-    piece(3)
-    piece(4)
-    expert_in(1)
-    expert_out(1, 0)
-    expert_out(1, 1)
-    for q in range(3):
-        ring_step(q, 4)
-        table_part(q)
-    steps((3, 1), (4, 1))
-    far_combine(0)
-    steps((3, 2), (4, 2))
-    table_mid(0)
-    far_combine(1)
-    steps((3, 3), (4, 3))
-    table_mid(1)
-    table_mid(2)
-    for q in (3, 4):
-        ring_step(q, 4)
-        table_part(q)
-
-    mix = mix_of(blend)
-    for part in range(2):
+    def far_inputs():
+        far_copy(0).wait_recv()
+        far_copy(1).wait_recv()
+        choose(far_meta[...], far_pick, far_blend)
+        dispatch(1, 0)
+        dispatch_sends(1, 0)
+
+    def far_grads():
+        far_copy(2).wait_recv()
+        dispatch(1, 1)
+        dispatch_sends(1, 1)
+
+    def own_grads():
+        dispatch(0, 1)
+        dispatch_sends(0, 1)
+
+    def own_sources():
+        select(mine)
+        select(theirs)
+
+    def weights_here():
+        all_bytes(up_buf.at[pl.ds(0, 4 * 2 * UPR)], x_recv.at[0])
+        all_bytes(down_buf.at[pl.ds(0, 4 * 2 * DNR)], x_recv.at[1])
+        for d in range(2):
+            for at in range(2):
+                wide_copy(d, at, FAR_Z - 1).wait_recv()
+
+    def combine(part):
+        mix = mix_of(blend)
         returned(0, part)
         back_copy(part).wait_recv()
 
@@ -459,10 +432,73 @@
             total = jnp.dot(mix, ret_got[0:SET, cols], preferred_element_type=F32)
             gi_ref[:, cols] = (total + far_back[:, cols].astype(F32)).astype(BF16)
 
-    for q in range(3):
-        table_sum(q)
+    piece(0)
+    own_grads()
+    steps(("weights", 1), ("meta", 1))
+    ring_step(0, 1)
+    own_sources()
+    sources(1)
+    far_inputs()
+    steps(("weights", 2), ("meta", 2))
+    ring_step(0, 2)
+    piece(1)
+    piece(2)
+    sources(2)
+    far_grads()
+    steps(("weights", 3), ("meta", 3))
+    ring_step(0, 3)
+    sources(3)
+    steps(("weights", 4), ("meta", 4))
+    wide_send(0)
+    wide_send(1)
+    sources(4)
+    ring_step(0, 4)
+    table_part(0)
+    ring_step(1, 1)
+    ring_step(2, 1)
+    weights_here()
+    expert_in(0)
+    ring_step(1, 2)
+    ring_step(2, 2)
+    expert_out(0, 0)
+    expert_send(0, 0)
+    ring_step(1, 3)
+    ring_step(2, 3)
+    piece(3)
+    piece(4)
+    expert_out(0, 1)
+    expert_in(1)
+    expert_out(1, 0)
+    expert_send(1, 0)
+    ring_step(1, 4)
+    expert_out(1, 1)
+    expert_send(1, 1)
+    expert_send(0, 1)
+    ring_step(2, 4)
+    ring_step(3, 1)
+    ring_step(4, 1)
+    table_part(1)
+    table_mid(0)
+    table_part(2)
+    ring_step(3, 2)
+    ring_step(4, 2)
+    table_mid(1)
+    ring_step(3, 3)
+    ring_step(4, 3)
+    far_combine(0)
+    table_mid(2)
+    ring_step(3, 4)
+    table_part(3)
+    ring_step(4, 4)
+    table_part(4)
+    far_combine(1)
     table_mid(3)
     table_mid(4)
+    combine(0)
+    combine(1)
+    table_sum(0)
+    table_sum(1)
+    table_sum(2)
     table_sum(3)
     table_sum(4)
 
@@ -539,7 +575,7 @@
             pltpu.VMEM((EXPERTS * CAP, D), BF16),
             pltpu.VMEM((EXPERTS * CAP, D), BF16),
             pltpu.VMEM((EXPERTS * CAP, D), BF16),
-            pltpu.VMEM((256, HID), BF16),
+            pltpu.VMEM((2, SET, HID), BF16),
             pltpu.VMEM((EXPERTS * CAP, D), BF16),
             pltpu.VMEM((EXPERTS * CAP, D), BF16),
             pltpu.VMEM((TOK, D), BF16),

time: 134 us -> 128 us (0.955)
  Pallas kernels: 127 us -> 121 us
    pallas_call x1, Pallas kernels: 127 us -> 121 us  [per_device(): pl.pallas_call(kernel, out_shape=(jax.ShapeDtypeStruct((TOK, D), BF16), j...]
where the time goes in v5:
time: 128 us
  Pallas kernels  121 us (95%)
  local copies, waits for them, and re-layouts  4.72 us (4%)
    pallas_call x1, Pallas kernels, per_device(): pl.pallas_call(kernel, out_shape=(jax.ShapeDtypeStruct((TOK, D), BF16), j...  121 us
    unnamed x14, local copies, waits for them, and re-layouts  4.62 us

profile of v5, /device:TPU:1, one launch (start us, length us, event | category | flops | bytes accessed | tf_op | source)
XLA Modules:
  0.0 127.6 jit_solution(10265763946170638193)
XLA Ops:
  0.6 0.0 copy-start.3
  0.6 0.0 copy-start.2
  0.7 0.1 pad.2.clone
  0.7 0.6 copy-done.3
  1.3 0.0 copy-done.2
  1.3 0.0 copy-start.4
  1.3 0.1 fusion.12
  1.4 0.6 copy-done.4
  2.0 0.0 copy-start.1
  2.0 0.0 copy-start.5
  2.1 0.7 copy-done.1
  2.7 0.0 copy-done.5
  2.7 0.7 maximum_maximum_fusion.meta_ref
  3.4 121.4 %shard_map.104 = (bf16[128,2560]{1,0:T(8,128)(2,1)}, f32[4,16,1280]{2,1,0:T(8,128)}) custom-call(bf16[128,2560]{1,0:T(8,128)(2,1)} %grad_ref.1, bf16[128,2560]{1,0:T(8,128)(2,1)} %input_ref.1, bf16[2,80,512]{2,1,0:T(8,128)(2,1)} %up_ref.1, bf16[2,16,2560]{2,1,0:T(8,128)(2,1)} %down_ref.1, f32[3,8,128]{2,1,0:T(8,128)} %maximum_maximum_fusion.meta_ref), custom_call_target="tpu_custom_call" | custom-call | flops 10000000000 | bytes 4000000 | tf_op jit(solution)/shard_map/pallas_call | solution.py:556
  124.8 0.0 copy-start
  124.8 2.0 %copy.13 = bf16[128,2560]{1,0:T(8,128)(2,1)} copy(bf16[128,2560]{1,0:T(8,128)(2,1)} %get-tuple-element.4) | data formatting | bytes 1310720
  126.8 0.0 copy-done
  126.8 0.7 copy.14
  (6 shorter events, 0.0 us)
Async XLA Ops:
  0.6 0.7 copy-start.3
  0.6 0.7 copy-start.2
  1.3 0.7 copy-start.4
  2.0 0.7 copy-start.1
  2.0 0.7 copy-start.5
  124.8 2.0 %copy-start = (f32[4,16,1280]{2,1,0:T(8,128)S(1)}, f32[4,16,1280]{2,1,0:T(8,128)}, u32[]{:S(2)}) copy-start(f32[4,16,1280]{2,1,0:T(8,128)} %get-tuple-element.5) | copy-start | bytes 983044

commit v6 on v5

--- a/solution.py
+++ b/solution.py
@@ -466,13 +466,13 @@
     ring_step(2, 3)
     piece(3)
     piece(4)
-    expert_out(0, 1)
     expert_in(1)
     expert_out(1, 0)
     expert_send(1, 0)
     ring_step(1, 4)
     expert_out(1, 1)
     expert_send(1, 1)
+    expert_out(0, 1)
     expert_send(0, 1)
     ring_step(2, 4)
     ring_step(3, 1)
@@ -492,13 +492,13 @@
     ring_step(4, 4)
     table_part(4)
     far_combine(1)
-    table_mid(3)
-    table_mid(4)
-    combine(0)
-    combine(1)
     table_sum(0)
     table_sum(1)
     table_sum(2)
+    table_mid(3)
+    combine(0)
+    table_mid(4)
+    combine(1)
     table_sum(3)
     table_sum(4)
 

time: 128 us -> 128 us (level)
  no operation moved by 1% of the time
where the time goes in v6:
time: 128 us
  Pallas kernels  121 us (95%)
  local copies, waits for them, and re-layouts  4.72 us (4%)
    pallas_call x1, Pallas kernels, per_device(): pl.pallas_call(kernel, out_shape=(jax.ShapeDtypeStruct((TOK, D), BF16), j...  121 us
    unnamed x14, local copies, waits for them, and re-layouts  4.62 us

profile of v6, /device:TPU:1, one launch (start us, length us, event | category | flops | bytes accessed | tf_op | source)
XLA Modules:
  0.0 127.5 jit_solution(4419919702630536842)
XLA Ops:
  0.6 0.0 copy-start.3
  0.6 0.0 copy-start.2
  0.7 0.1 pad.2.clone
  0.7 0.6 copy-done.3
  1.3 0.0 copy-done.2
  1.3 0.0 copy-start.4
  1.3 0.1 fusion.12
  1.4 0.6 copy-done.4
  2.0 0.0 copy-start.1
  2.0 0.0 copy-start.5
  2.1 0.7 copy-done.1
  2.7 0.0 copy-done.5
  2.7 0.7 maximum_maximum_fusion.meta_ref
  3.4 121.3 %shard_map.104 = (bf16[128,2560]{1,0:T(8,128)(2,1)}, f32[4,16,1280]{2,1,0:T(8,128)}) custom-call(bf16[128,2560]{1,0:T(8,128)(2,1)} %grad_ref.1, bf16[128,2560]{1,0:T(8,128)(2,1)} %input_ref.1, bf16[2,80,512]{2,1,0:T(8,128)(2,1)} %up_ref.1, bf16[2,16,2560]{2,1,0:T(8,128)(2,1)} %down_ref.1, f32[3,8,128]{2,1,0:T(8,128)} %maximum_maximum_fusion.meta_ref), custom_call_target="tpu_custom_call" | custom-call | flops 10000000000 | bytes 4000000 | tf_op jit(solution)/shard_map/pallas_call | solution.py:556
  124.8 0.0 copy-start
  124.8 2.0 %copy.13 = bf16[128,2560]{1,0:T(8,128)(2,1)} copy(bf16[128,2560]{1,0:T(8,128)(2,1)} %get-tuple-element.4) | data formatting | bytes 1310720
  126.8 0.0 copy-done
  126.8 0.7 copy.14
  (6 shorter events, 0.0 us)
Async XLA Ops:
  0.6 0.7 copy-start.3
  0.6 0.7 copy-start.2
  1.3 0.7 copy-start.4
  2.0 0.7 copy-start.1
  2.0 0.7 copy-start.5
  124.8 2.0 %copy-start = (f32[4,16,1280]{2,1,0:T(8,128)S(1)}, f32[4,16,1280]{2,1,0:T(8,128)}, u32[]{:S(2)}) copy-start(f32[4,16,1280]{2,1,0:T(8,128)} %get-tuple-element.5) | copy-start | bytes 983044

commit v7 on v6

--- a/solution.py
+++ b/solution.py
@@ -47,7 +47,7 @@
     grad_ref, input_ref, up_ref, down_ref, meta_ref,
     gi_ref, table_ref,
     up_buf, down_buf, far_x, far_g, far_meta, pick, far_pick, blend, far_blend,
-    send_x, send_g, got_x, got_g, slope_buf, ret_send, ret_got, far_out, far_back,
+    send_x, send_g, got_x, got_g, pre_buf, slope_buf, ret_send, ret_got, far_out, far_back,
     gbuf, mbuf, sel, dense, s1_got, s2_send, s2_got,
     pre_recv, pre_send, w_recv, w_send, x_recv, x2_recv, x_send, e_recv, e_send, m_recv, m_send, t_recv, t_send,
     f_recv, f_send, d_recv, d_send, r_recv, r_send, b_recv, b_send, s1_recv, s1_send, s2_recv, s2_send_sem,
@@ -286,15 +286,25 @@
     def others(group):
         return pl.ds(group * SET, (PEERS - 1) * CAP)
 
-    def expert_in(group):
+    def expert_pre(group):
         all_bytes(got_x.at[others(group)], d_recv.at[group, 0])
-        all_bytes(got_g.at[others(group)], d_recv.at[group, 1])
         rows = pl.ds(group * SET, SET)
 
         @pl.loop(0, 2)
         def _(n):
             cols = pl.ds(pl.multiple_of(n * 256, 256), 256)
-            before = jnp.dot(got_x[rows, :], up_buf[:, cols], preferred_element_type=F32)
+            pre_buf[:, cols] = jnp.dot(
+                got_x[rows, :], up_buf[:, cols], preferred_element_type=F32
+            )
+
+    def expert_in(group):
+        all_bytes(got_g.at[others(group)], d_recv.at[group, 1])
+        rows = pl.ds(group * SET, SET)
+
+        @pl.loop(0, 2)
+        def _(n):
+            cols = pl.ds(pl.multiple_of(n * 256, 256), 256)
+            before = pre_buf[:, cols]
             back = nt_dot(got_g[rows, :], down_buf[cols, :])
             sig = 1.0 / (1.0 + jnp.exp(-before))
             slope_buf[group, :, cols] = (back * sig * (1.0 + before * (1.0 - sig))).astype(BF16)
@@ -457,7 +467,9 @@
     ring_step(1, 1)
     ring_step(2, 1)
     weights_here()
+    expert_pre(0)
     expert_in(0)
+    expert_pre(1)
     ring_step(1, 2)
     ring_step(2, 2)
     expert_out(0, 0)
@@ -575,6 +587,7 @@
             pltpu.VMEM((EXPERTS * CAP, D), BF16),
             pltpu.VMEM((EXPERTS * CAP, D), BF16),
             pltpu.VMEM((EXPERTS * CAP, D), BF16),
+            pltpu.VMEM((SET, HID), F32),
             pltpu.VMEM((2, SET, HID), BF16),
             pltpu.VMEM((EXPERTS * CAP, D), BF16),
             pltpu.VMEM((EXPERTS * CAP, D), BF16),

time: 128 us -> 128 us (level)
  no operation moved by 1% of the time
where the time goes in v7:
time: 128 us
  Pallas kernels  122 us (95%)
  local copies, waits for them, and re-layouts  4.72 us (4%)
    pallas_call x1, Pallas kernels, per_device(): pl.pallas_call(kernel, out_shape=(jax.ShapeDtypeStruct((TOK, D), BF16), j...  122 us
    unnamed x14, local copies, waits for them, and re-layouts  4.62 us

profile of v7, /device:TPU:1, one launch (start us, length us, event | category | flops | bytes accessed | tf_op | source)
XLA Modules:
  0.0 127.7 jit_solution(3812104325058699427)
XLA Ops:
  0.6 0.0 copy-start.3
  0.6 0.0 copy-start.2
  0.7 0.1 pad.2.clone
  0.7 0.6 copy-done.3
  1.3 0.0 copy-done.2
  1.3 0.0 copy-start.4
  1.3 0.1 fusion.12
  1.4 0.6 copy-done.4
  2.0 0.0 copy-start.1
  2.0 0.0 copy-start.5
  2.1 0.7 copy-done.1
  2.7 0.0 copy-done.5
  2.7 0.7 maximum_maximum_fusion.meta_ref
  3.4 121.5 %shard_map.104 = (bf16[128,2560]{1,0:T(8,128)(2,1)}, f32[4,16,1280]{2,1,0:T(8,128)}) custom-call(bf16[128,2560]{1,0:T(8,128)(2,1)} %grad_ref.1, bf16[128,2560]{1,0:T(8,128)(2,1)} %input_ref.1, bf16[2,80,512]{2,1,0:T(8,128)(2,1)} %up_ref.1, bf16[2,16,2560]{2,1,0:T(8,128)(2,1)} %down_ref.1, f32[3,8,128]{2,1,0:T(8,128)} %maximum_maximum_fusion.meta_ref), custom_call_target="tpu_custom_call" | custom-call | flops 10000000000 | bytes 4000000 | tf_op jit(solution)/shard_map/pallas_call | solution.py:568
  124.9 0.0 copy-start
  124.9 2.0 %copy.13 = bf16[128,2560]{1,0:T(8,128)(2,1)} copy(bf16[128,2560]{1,0:T(8,128)(2,1)} %get-tuple-element.4) | data formatting | bytes 1310720
  127.0 0.0 copy-done
  127.0 0.7 copy.14
  (6 shorter events, 0.0 us)
Async XLA Ops:
  0.6 0.7 copy-start.3
  0.6 0.7 copy-start.2
  1.3 0.7 copy-start.4
  2.0 0.7 copy-start.1
  2.0 0.7 copy-start.5
  124.9 2.0 %copy-start = (f32[4,16,1280]{2,1,0:T(8,128)S(1)}, f32[4,16,1280]{2,1,0:T(8,128)}, u32[]{:S(2)}) copy-start(f32[4,16,1280]{2,1,0:T(8,128)} %get-tuple-element.5) | copy-start | bytes 983044
